TPU v7x, 32 devices: a whole 2x2x4 slice. The times are simulated.
32 devices in a mesh: seq: 8 (over z, y), head: 4 (over x, core).
Axes of the slice: x: 2, y: 2, z: 4, core: 2. Of those that a mesh axis runs over, the one named last changes fastest.
Arguments:
- tokens: bfloat16 [14112, 384], P(('seq', 'head')), may hold values from -6 to 6
- actions: bfloat16 [24, 3, 384], P('seq'), may hold values from -6 to 6
- action_mask: int32 [24, 3], P('seq'), may hold values 0 or 1
- frame_mask: int32 [24, 3, 3], P('seq'), may hold values from 0 to 1, as said below
- environment_id: int32 [24], P('seq'), may hold values from 0 to 7
- environment_embed: float32 [8, 384], replicated, may hold values from -3 to 3
- norm_gain: float32 [2, 2, 384], replicated, may hold values from 0.25 to 1.75
- norm_bias: float32 [2, 2, 384], replicated, may hold values from -2 to 2
- input_weight: bfloat16 [2, 3, 384, 1024], P(None, None, None, 'head'), may hold values from -0.3125 to 0.3125
- output_weight: bfloat16 [2, 1024, 384], P(None, 'head'), may hold values from -1.5 to 1.5
- output_bias: float32 [2, 384], replicated, may hold values from -2 to 2
- up_weight: bfloat16 [2, 384, 2048], replicated, may hold values from -0.3125 to 0.3125
- up_bias: float32 [2, 2048], replicated, may hold values from -3 to 3
- down_weight: bfloat16 [2, 2048, 384], replicated, may hold values from -0.25 to 0.25
- down_bias: float32 [2, 384], replicated, may hold values from -2 to 2
- cotangent: bfloat16 [14112, 384], P(('seq', 'head')), may hold values from -6 to 6
Outputs:
- mixed: bfloat16 [14112, 384], P(('seq', 'head'))
- tokens_gradient: float32 [14112, 384], P(('seq', 'head'))
- environment_gradient: float32 [8, 384], replicated
- gain_gradient: float32 [2, 2, 384], replicated
- bias_gradient: float32 [2, 2, 384], replicated
- input_weight_gradient: float32 [2, 3, 384, 1024], P(None, None, None, 'head')
- output_weight_gradient: float32 [2, 1024, 384], P(None, 'head')
- output_bias_gradient: float32 [2, 384], replicated
- up_weight_gradient: float32 [2, 384, 2048], replicated
- up_bias_gradient: float32 [2, 2048], replicated
- down_weight_gradient: float32 [2, 2048, 384], replicated
- down_bias_gradient: float32 [2, 384], replicated
Inputs may be any that keep to these rules, and one draw needn't show every extreme that they name: frame_mask[s, f, f] = 1 and frame_mask[s, f, g] = 0 for g > f: a frame never reads a later one and always reads itself; earlier frames may be hidden.
All inputs are finite; a program needn't handle non-finite values. No bound on the sum of `action_mask` on one device may be relied on, other than what follows from the above.
Results may differ from a plain program's by a relative error of at most 0.018.
Values may be sent and summed in bfloat16 or wider, within the bound.
No kernel may reach another device: no remote copies, remote signals or barrier semaphores. Data moves between devices by JAX's collectives and lax.ppermute only.
A program may use at most 192 MiB of HBM per device.

v0:
```python
import functools
import math

import jax
import jax.numpy as jnp
from jax import lax
from jax.experimental import pallas as pl
from jax.experimental.pallas import tpu as pltpu
from jax.sharding import PartitionSpec as P

HEAD_DIM = 64
EPSILON = 1e-05
MASKED = -1e30
LOG2E = math.log2(math.e)
LN2 = math.log(2.0)
LANES = 128
BF16 = jnp.bfloat16
F32 = jnp.float32
NT = (((1,), (1,)), ((), ()))
NN = (((1,), (0,)), ((), ()))
TN = (((0,), (0,)), ((), ()))
MIB = 1024 * 1024
SMEM = pltpu.MemorySpace.SMEM


def up_to(value, step):
    return -(-value // step) * step


def dot(a, b, dims=NN):
    return lax.dot_general(a, b, dims, preferred_element_type=F32)


class Plan:
    def __init__(self, rows, groups, seqs, frames, width, local_width, hidden):
        self.rows, self.groups, self.seqs, self.frames = rows, groups, seqs, frames
        self.width, self.local, self.hidden = width, local_width, hidden
        self.block = up_to(rows, 16)
        self.total = self.block * groups
        self.length = rows * groups // seqs
        self.patches = self.length // frames
        self.heads = local_width // HEAD_DIM
        self.group_lanes = LANES // self.heads
        place = lambda t: t // rows * self.block + t % rows
        starts = [place(s * self.length) // 16 * 16 for s in range(seqs)]
        ends = [place((s + 1) * self.length - 1) + 1 for s in range(seqs)]
        self.window = max(up_to(e - s, 16) for s, e in zip(starts, ends))
        self.stride = starts[1] - starts[0]
        assert seqs == 3 and groups == 4
        assert starts == [self.stride * s for s in range(seqs)]
        assert self.window <= 2 * self.block
        assert starts[-1] + self.window <= self.total
        self.lanes = up_to(self.window, LANES)
        first = [
            min(place(s * self.length + f * self.patches) - starts[s] for s in range(seqs))
            for f in range(frames)
        ]
        last = [
            max(
                place(s * self.length + (f + 1) * self.patches - 1) - starts[s] + 1
                for s in range(seqs)
            )
            for f in range(frames)
        ]
        self.cuts = [first[f] // 16 * 16 if f else 0 for f in range(frames)] + [self.window]
        ends = [0] + [min(up_to(last[f], LANES), self.lanes) for f in range(frames - 1)] + [self.lanes]
        self.key_chunks = [
            (ends[f], ends[f + 1] - ends[f], self.cuts[f]) for f in range(frames)
        ]
        begins = [first[f] // LANES * LANES if f else 0 for f in range(frames)] + [self.lanes]
        reach = [up_to(last[f], 16) for f in range(frames - 1)] + [self.window]
        self.query_chunks = [
            (begins[f], begins[f + 1] - begins[f], reach[f]) for f in range(frames)
        ]

    def sequence(self, slot, across):
        if slot == 2:
            return 1
        return across * (self.seqs - 1) if slot == 0 else (1 - across) * (self.seqs - 1)


def params(mib):
    return pltpu.CompilerParams(vmem_limit_bytes=mib * MIB)


def result(shape, dtype, away=False):
    return pltpu.HBM(shape, dtype) if away else jax.ShapeDtypeStruct(shape, dtype)


def far(arrays, away=True):
    return [pltpu.with_memory_space_constraint(a, pltpu.HBM) if away else a for a in arrays]


def cost(microseconds):
    return pl.CostEstimate(flops=0, bytes_accessed=int(3.69e6 * microseconds), transcendentals=0)


def full(shape):
    return pl.BlockSpec(shape, lambda *i: (0,) * len(shape))


def layer_of(shape, layer):
    return pl.BlockSpec((None,) + shape, lambda *i: (layer,) + (0,) * len(shape))


def norm_stats(values):
    center = values - jnp.mean(values, axis=-1, keepdims=True)
    spread = jnp.mean(center * center, axis=-1, keepdims=True)
    return center, lax.rsqrt(spread + EPSILON)


def norm_back(upstream, center, scale, gain):
    unit = center * scale
    weighted = upstream * gain
    mean_w = jnp.mean(weighted, axis=-1, keepdims=True)
    mean_wn = jnp.mean(weighted * unit, axis=-1, keepdims=True)
    grad = scale * (weighted - mean_w - unit * mean_wn)
    return (
        grad,
        jnp.sum(upstream * unit, axis=0, keepdims=True),
        jnp.sum(upstream, axis=0, keepdims=True),
    )


def prologue_kernel(
    plan, me_ref, act_mask, frame_mask, env_id, tokens, actions, embed, gain, shift, stream, normed, qhot, kbias, valid
):
    rows, block = plan.rows, plan.block
    row = lax.broadcasted_iota(jnp.int32, (block, plan.width), 0)
    place = me_ref[0] * rows + row
    condition = jnp.zeros((block, plan.width), F32)
    for s in range(plan.seqs):
        env = jnp.zeros((1, plan.width), F32)
        for e in range(embed.shape[0]):
            env = jnp.where(env_id[0:1, s : s + 1] == e, embed[e : e + 1, :], env)
        for f in range(plan.frames):
            mask = act_mask[s : s + 1, f : f + 1].astype(F32)
            term = actions[s, f : f + 1, :].astype(F32) * mask + env
            begin = s * plan.length + f * plan.patches
            condition = jnp.where(
                (place >= begin) & (place < begin + plan.patches), term, condition
            )
    padded = jnp.concatenate(
        [tokens[...].astype(F32), jnp.zeros((block - rows, plan.width), F32)], axis=0
    )
    values = jnp.where(row < rows, padded + condition, 0.0)
    stream[...] = values
    center, scale = norm_stats(values)
    normed[...] = (center * scale * gain[0:1, :] + shift[0:1, :]).astype(BF16)
    line = lax.broadcasted_iota(jnp.int32, (plan.lanes, LANES), 0)
    lane = lax.broadcasted_iota(jnp.int32, (plan.lanes, LANES), 1) % plan.group_lanes
    for slot in range(plan.seqs):
        s = plan.sequence(slot, me_ref[0] // 2)
        at = plan.stride * s + line
        origin = at
        inside = line < plan.window
        for b in range(plan.groups):
            here = (at >= b * block) & (at < (b + 1) * block)
            origin = jnp.where(here, at - b * (block - rows), origin)
            inside = inside & jnp.logical_not(here & (at >= b * block + rows))
        token = origin - s * plan.length
        inside = inside & (token >= 0) & (token < plan.length)
        frame = jnp.zeros_like(token)
        for f in range(1, plan.frames):
            frame = frame + jnp.where(token >= f * plan.patches, 1, 0)
        frame = jnp.where(inside, frame, -1)
        qhot[slot] = jnp.where((lane == frame) & inside, 1.0, 0.0).astype(BF16)
        valid[slot] = jnp.where(inside, 1.0, 0.0)[: plan.window].astype(BF16)
        bias = jnp.where(lane < plan.frames, MASKED, 0.0)
        bias = jnp.where((lane >= plan.frames) & (lane < plan.frames + 3), 1.0, bias)
        allowed = frame_mask[s]
        for f in range(plan.frames):
            for g in range(plan.frames):
                value = jnp.where(allowed[f : f + 1, g : g + 1] > 0, 0.0, MASKED)
                bias = jnp.where((lane == f) & (frame == g), value, bias)
        kbias[slot] = bias.astype(BF16)


def prologue(plan, me, action_mask, frame_mask, env_id, tokens, actions, embed, gain, shift):
    return pl.pallas_call(
        functools.partial(prologue_kernel, plan),
        grid=(1,),
        in_specs=[pl.BlockSpec(memory_space=SMEM)]
        + [full(action_mask.shape), full(frame_mask.shape), full(env_id.shape)]
        + [full(tokens.shape), full(actions.shape), full(embed.shape)]
        + [layer_of(gain.shape[1:], 0), layer_of(gain.shape[1:], 0)],
        out_specs=[
            full((plan.block, plan.width)),
            full((plan.block, plan.width)),
            full((plan.seqs, plan.lanes, LANES)),
            full((plan.seqs, plan.lanes, LANES)),
            full((plan.seqs, plan.window, LANES)),
        ],
        out_shape=[
            jax.ShapeDtypeStruct((plan.block, plan.width), F32),
            jax.ShapeDtypeStruct((plan.block, plan.width), BF16),
            result((plan.seqs, plan.lanes, LANES), BF16),
            result((plan.seqs, plan.lanes, LANES), BF16),
            result((plan.seqs, plan.window, LANES), BF16),
        ],
        compiler_params=params(16),
        cost_estimate=cost(5),
        name="prologue",
    )(me, *far([action_mask, frame_mask, env_id, tokens, actions, embed, gain, shift]))


def place_blocks(plan, me, blocks, target):
    x, c = me[0] // 2, me[0] % 2
    if len(blocks) == 2:
        order = [c, 1 - c]
    else:
        order = [2 * x + c, 2 * x + 1 - c, 2 * (1 - x) + c, 2 * (1 - x) + 1 - c]
    for ref, b in zip(blocks, order):
        target[pl.ds(pl.multiple_of(b * plan.block, 16), plan.block), :] = ref[...]


def scatter_blocks(plan, me, block_of, outs):
    x, c = me[0] // 2, me[0] % 2
    order = [2 * (1 - x) + 1 - c, 2 * x + 1 - c, 2 * (1 - x) + c, 2 * x + c]
    for ref, b in zip(outs, order):
        rows = pl.ds(pl.multiple_of(b * plan.block, 16), plan.block)
        ref[...] = block_of(rows).astype(BF16)


def window_start(plan, me, slots, blocks):
    x = me[0] // 2
    if len(slots) == 1:
        s = plan.sequence(slots[0], x)
    else:
        s = jnp.int32(0)
        for i, slot in enumerate(slots):
            s = jnp.where(pl.program_id(0) == i, plan.sequence(slot, x), s)
    start = s * plan.stride
    if blocks == 2:
        start = start - x * (2 * plan.block)
    return pl.multiple_of(start, 16)


def group_mask(plan, head):
    lane = lax.broadcasted_iota(jnp.int32, (1, LANES), 1)
    return jnp.where(lane // plan.group_lanes == head, 1.0, 0.0).astype(BF16)


def put_windows(plan, me, slots, before, target, value):
    over = plan.window - plan.stride
    step = pl.program_id(0)
    at = window_start(plan, me, slots, 4)

    @pl.when(step == 0)
    def _():
        target[...] = jnp.zeros(target.shape, target.dtype)
        for slot, ref in enumerate(before):
            start = pl.multiple_of(plan.sequence(slot, me[0] // 2) * plan.stride, 16)
            target[pl.ds(start, plan.window), :] = ref[0]

    inner = pl.ds(pl.multiple_of(at + over, 16), plan.window - 2 * over)
    target[inner, :] = value[over : plan.window - over]
    for begin in (0, plan.window - over):
        rows = pl.ds(pl.multiple_of(at + begin, 16), over)
        target[rows, :] = target[rows, :] + value[begin : begin + over]


def attend_kernel(plan, slots, blocks, *refs):
    me, refs = refs[0], refs[1:]
    placed, refs = refs[:blocks], refs[blocks:]
    w_in, qhot, kbias, valid = refs[:4]
    refs = refs[4:]
    last = blocks == 4
    if last:
        w_out, before, refs = refs[0], refs[1], refs[2:]
    triple, attention, lse = refs[:3]
    refs = refs[3:]
    if last:
        outs, refs = refs[:4], refs[4:]
    gathered, q_even, q_odd, keys, values, *whole = refs
    window, local = plan.window, plan.local

    @pl.when(pl.program_id(0) == 0)
    def _():
        place_blocks(plan, me, placed, gathered)
        keys[window:, :] = jnp.zeros((plan.lanes - window, local), BF16)
        values[window:, :] = jnp.zeros((plan.lanes - window, local), BF16)

    x = gathered[pl.ds(window_start(plan, me, slots, blocks), window), :]
    query = dot(x, w_in[0]) * (HEAD_DIM ** (-0.5) * LOG2E)
    odd_lane = lax.broadcasted_iota(jnp.int32, (1, local), 1) // HEAD_DIM % 2 == 1
    q_even[...] = jnp.where(odd_lane, 0.0, query).astype(BF16)
    q_odd[...] = jnp.where(odd_lane, query, 0.0).astype(BF16)
    triple[0, :, 0:local] = query.astype(BF16)
    key = dot(x, w_in[1]).astype(BF16)
    triple[0, :, local : 2 * local] = key
    keys[0:window, :] = key
    value = dot(x, w_in[2]).astype(BF16)
    triple[0, :, 2 * local : 3 * local] = value
    values[0:window, :] = value
    left = lax.broadcasted_iota(jnp.int32, (1, LANES), 1) < HEAD_DIM
    lane_head = lax.broadcasted_iota(jnp.int32, (1, LANES), 1) // plan.group_lanes
    chunks = plan.key_chunks
    spans = list(zip(plan.cuts[:-1], plan.cuts[1:]))

    def scores_of(head):
        cols = slice(head // 2 * LANES, (head // 2 + 1) * LANES)
        q = (q_even, q_odd)[head % 2]
        pick = group_mask(plan, head)
        scores = []
        for k0, count, r0 in chunks:
            lhs = jnp.concatenate([q[r0:, cols], qhot[0, r0:window, :]], axis=1)
            rhs = jnp.concatenate(
                [keys[k0 : k0 + count, cols], kbias[0, k0 : k0 + count, :] * pick], axis=1
            )
            scores.append(dot(lhs, rhs, NT))
        return scores

    def soften(scores):
        tops, weights = [], [[] for _ in chunks]
        for i, (begin, end) in enumerate(spans):
            pieces = [scores[c][begin - chunks[c][2] : end - chunks[c][2]] for c in range(i + 1)]
            top = jnp.max(jnp.concatenate(pieces, axis=1), axis=-1, keepdims=True)
            tops.append(jnp.broadcast_to(top, (end - begin, LANES)))
            for c in range(i + 1):
                weights[c].append(jnp.exp2(pieces[c] - top).astype(BF16))
        return jnp.concatenate(tops, axis=0), [jnp.concatenate(w, axis=0) for w in weights]

    def mix(head, weights):
        cols = slice(head // 2 * LANES, (head // 2 + 1) * LANES)
        parts = []
        for (k0, count, _), weight in zip(chunks, weights):
            rhs = jnp.concatenate(
                [values[k0 : k0 + count, cols], jnp.ones((count, LANES), BF16)], axis=1
            )
            parts.append(dot(weight, rhs))
        rows = []
        for i, (begin, end) in enumerate(spans):
            pieces = [parts[c][begin - chunks[c][2] : end - chunks[c][2]] for c in range(i + 1)]
            rows.append(functools.reduce(jnp.add, pieces))
        return jnp.concatenate(rows, axis=0)

    state = {}

    def finish(head, top, mixed):
        total = mixed[:, LANES:]
        state[head] = mixed[:, :LANES] / total
        if head == 0:
            state["top"], state["total"] = top, total
        else:
            state["top"] = jnp.where(lane_head == head, top, state["top"])
            state["total"] = jnp.where(lane_head == head, total, state["total"])
        if head % 2 == 1:
            both = jnp.where(left, state[head - 1], state[head]) * valid[0].astype(F32)
            attention[0, :, (head // 2) * LANES : (head // 2 + 1) * LANES] = both.astype(BF16)

    heads = plan.heads
    scores = {h: scores_of(h) for h in range(min(2, heads))}
    soft, mixed = {}, {}
    for h in range(heads):
        soft[h] = soften(scores.pop(h))
        if h + 2 < heads:
            scores[h + 2] = scores_of(h + 2)
        mixed[h] = mix(h, soft[h][1])
        if h >= 1:
            finish(h - 1, soft[h - 1][0], mixed.pop(h - 1))
    finish(heads - 1, soft[heads - 1][0], mixed.pop(heads - 1))
    lse[0] = state["top"] + jnp.log2(state["total"])
    if last:
        put_windows(plan, me, slots, [before], whole[0], attention[0])

        @pl.when(pl.program_id(0) == len(slots) - 1)
        def _():
            scatter_blocks(plan, me, lambda rows: dot(whole[0][rows, :], w_out[...]), outs)


def per_slot(slots, shape):
    first = slots[0]
    return pl.BlockSpec((1,) + shape, lambda s: (s + first,) + (0,) * len(shape))


def attend(plan, layer, slots, me, blocks, input_weight, masks, away, output_weight=None, before=None):
    block = (plan.block, plan.width)
    n = len(slots)
    last = before is not None
    each = lambda shape: pl.BlockSpec((1,) + shape, lambda s: (s, 0, 0))
    shape = lambda *dims: result((n, plan.window) + dims, BF16, away)
    in_specs = [pl.BlockSpec(memory_space=SMEM)] + [full(block)] * len(blocks)
    in_specs += [layer_of(input_weight.shape[1:], layer)]
    in_specs += [per_slot(slots, m.shape[1:]) for m in masks]
    out_specs = [
        each((plan.window, 3 * plan.local)),
        each((plan.window, plan.local)),
        each((plan.window, LANES)),
    ]
    out_shape = [
        shape(3 * plan.local),
        shape(plan.local),
        result((n, plan.window, LANES), F32, away),
    ]
    scratch = [
        pltpu.VMEM((len(blocks) * plan.block, plan.width), BF16),
        pltpu.VMEM((plan.window, plan.local), BF16),
        pltpu.VMEM((plan.window, plan.local), BF16),
        pltpu.VMEM((plan.lanes, plan.local), BF16),
        pltpu.VMEM((plan.lanes, plan.local), BF16),
    ]
    args = [me, *blocks, input_weight, *masks]
    if last:
        in_specs += [layer_of(output_weight.shape[1:], layer), full(before.shape)]
        args += [output_weight, before]
        out_specs += [full(block)] * 4
        out_shape += [jax.ShapeDtypeStruct(block, BF16)] * 4
        scratch += [pltpu.VMEM((plan.total, plan.local), BF16)]
    area = plan.window * plan.lanes * plan.heads
    return pl.pallas_call(
        functools.partial(attend_kernel, plan, slots, len(blocks)),
        grid=(n,),
        in_specs=in_specs,
        out_specs=out_specs,
        out_shape=out_shape,
        scratch_shapes=scratch,
        compiler_params=params(20),
        cost_estimate=cost(3 * n),
        name="attend",
    )(*args)


def three_parts(value):
    high = value.astype(BF16)
    rest = value - high.astype(F32)
    middle = rest.astype(BF16)
    low = (rest - middle.astype(F32)).astype(BF16)
    return high.astype(F32), middle.astype(F32), low.astype(F32)


def attend_back_kernel(plan, slots, blocks, *refs):
    me, refs = refs[0], refs[1:]
    placed, refs = refs[:blocks], refs[blocks:]
    w_out, qhot, kbias, valid, triple, attention, lse = refs[:7]
    refs = refs[7:]
    last = slots[-1] == plan.seqs - 1
    if last:
        w_in, before, refs = refs[0], refs[1 : 1 + slots[0]], refs[1 + slots[0] :]
    triple_grad, refs = refs[0], refs[1:]
    if last:
        outs, refs = refs[:4], refs[4:]
    gathered, queries, grads, query_side, grad_side, key_turned, *whole = refs
    window, local, lanes = plan.window, plan.local, plan.lanes

    @pl.when(pl.program_id(0) == 0)
    def _():
        place_blocks(plan, me, placed, gathered)
        queries[window:, :] = jnp.zeros((lanes - window, local), BF16)
        grads[window:, :] = jnp.zeros((lanes - window, local), BF16)
        query_side[window:, :] = jnp.zeros((lanes - window, LANES), BF16)
        grad_side[window:, :] = jnp.zeros((lanes - window, LANES), BF16)

    mask = valid[0].astype(F32)
    head_grad = dot(gathered[pl.ds(window_start(plan, me, slots, blocks), window), :], w_out[...], NT)
    head_grad = head_grad * jnp.concatenate([mask] * (local // LANES), axis=1)
    head_grad = head_grad.astype(BF16)
    grads[0:window, :] = head_grad
    queries[0:window, :] = triple[0, :, 0:local]
    key_turned[...] = triple[0, :, local : 2 * local].T
    product = head_grad.astype(F32) * attention[0].astype(F32)
    high = product.astype(BF16)
    low = (product - high.astype(F32)).astype(BF16)
    spread = jnp.where(
        lax.broadcasted_iota(jnp.int32, (local, LANES), 0) // HEAD_DIM
        == lax.broadcasted_iota(jnp.int32, (local, LANES), 1) // plan.group_lanes,
        1.0,
        0.0,
    ).astype(BF16)
    inner = dot(high, spread) + dot(low, spread)
    slot = lax.broadcasted_iota(jnp.int32, (1, LANES), 1) % plan.group_lanes
    a, b, c = three_parts(-inner)
    grad_side[0:window, :] = jnp.where(
        slot == 0, a, jnp.where(slot == 1, b, jnp.where(slot == 2, c, 0.0))
    ).astype(BF16)
    a, b, c = three_parts(-lse[0])
    n = plan.frames
    query_side[0:window, :] = jnp.where(
        slot < n,
        qhot[0, 0:window, :].astype(F32),
        jnp.where(slot == n, a, jnp.where(slot == n + 1, b, jnp.where(slot == n + 2, c, 0.0))),
    ).astype(BF16)
    left = lax.broadcasted_iota(jnp.int32, (1, LANES), 1) < HEAD_DIM
    sides = [jnp.where(left, 1.0, 0.0).astype(BF16), jnp.where(left, 0.0, 1.0).astype(BF16)]
    chunks = plan.query_chunks
    ends = [0] + [c[2] for c in chunks]

    def products(head):
        half = head % 2
        tile = head // 2 * LANES
        cols = slice(tile, tile + LANES)
        pick = group_mask(plan, head)
        ones = jnp.where(slot < 3, pick.astype(F32), 0.0).astype(BF16)
        key_side = jnp.concatenate(
            [
                triple[0, :, local + tile : local + tile + LANES] * sides[half],
                kbias[0, 0:window, :] * pick,
            ],
            axis=1,
        )
        value_side = jnp.concatenate(
            [
                triple[0, :, 2 * local + tile : 2 * local + tile + LANES] * sides[half],
                jnp.broadcast_to(ones, (window, LANES)),
            ],
            axis=1,
        )
        scores, prob_grads = [], []
        for q0, count, reach in chunks:
            rows = slice(q0, q0 + count)
            rhs = jnp.concatenate([queries[rows, cols], query_side[rows, :]], axis=1)
            scores.append(dot(key_side[:reach], rhs, NT))
        for q0, count, reach in chunks:
            rows = slice(q0, q0 + count)
            rhs = jnp.concatenate([grads[rows, cols], grad_side[rows, :]], axis=1)
            prob_grads.append(dot(value_side[:reach], rhs, NT))
        return scores, prob_grads

    def pointwise(scores, prob_grads):
        probs = [jnp.exp2(s) for s in scores]
        score_grads = [(p * g).astype(BF16) for p, g in zip(probs, prob_grads)]
        return [p.astype(BF16) for p in probs], score_grads

    def add_rows(parts):
        rows = []
        for i in range(len(chunks)):
            pieces = [p[ends[i] : ends[i + 1]] for p in parts[i:]]
            rows.append(functools.reduce(jnp.add, pieces))
        return jnp.concatenate(rows, axis=0)

    def gradients(head, probs, score_grads):
        tile = head // 2 * LANES
        cols = slice(tile, tile + LANES)
        value_parts, key_parts, query_parts = [], [], []
        turned = key_turned[tile + head % 2 * HEAD_DIM : tile + (head % 2 + 1) * HEAD_DIM, :]
        for (q0, count, reach), prob in zip(chunks, probs):
            value_parts.append(dot(prob, grads[q0 : q0 + count, cols]))
        for (q0, count, reach), score_grad in zip(chunks, score_grads):
            key_parts.append(dot(score_grad, queries[q0 : q0 + count, cols]))
        for (q0, count, reach), score_grad in zip(chunks, score_grads):
            query_parts.append(dot(turned[:, :reach], score_grad))
        return jnp.concatenate(query_parts, axis=1), add_rows(key_parts), add_rows(value_parts)

    heads = plan.heads
    found = [products(h) for h in range(heads)]
    pointed = [pointwise(*f) for f in found]
    for tile in range(heads // 2):
        even, odd = (gradients(h, *pointed[h]) for h in (2 * tile, 2 * tile + 1))
        query = jnp.concatenate([even[0], odd[0]], axis=0).T[:window] * HEAD_DIM ** (-0.5)
        key = jnp.where(left, even[1], odd[1]) * LN2
        value = jnp.where(left, even[2], odd[2])
        for t, grad in enumerate((query, key, value)):
            at = t * local + tile * LANES
            triple_grad[0, :, at : at + LANES] = grad.astype(BF16)
    if last:
        put_windows(plan, me, slots, before, whole[0], triple_grad[0])

        @pl.when(pl.program_id(0) == len(slots) - 1)
        def _():
            def back(rows):
                total = dot(whole[0][rows, 0:local], w_in[0], NT)
                for t in (1, 2):
                    total = total + dot(whole[0][rows, t * local : (t + 1) * local], w_in[t], NT)
                return total

            scatter_blocks(plan, me, back, outs)


def attend_back(plan, layer, slots, me, blocks, output_weight, masks, saved, away, input_weight=None, before=None):
    block = (plan.block, plan.width)
    n = len(slots)
    last = before is not None
    each = lambda shape: pl.BlockSpec((1,) + shape, lambda s: (s, 0, 0))
    in_specs = [pl.BlockSpec(memory_space=SMEM)] + [full(block)] * len(blocks)
    in_specs += [layer_of(output_weight.shape[1:], layer)]
    in_specs += [per_slot(slots, m.shape[1:]) for m in masks]
    in_specs += [per_slot([max(slots[0] - 1, 0)], a.shape[1:]) for a in saved]
    out_specs = [each((plan.window, 3 * plan.local))]
    out_shape = [jax.ShapeDtypeStruct((n, plan.window, 3 * plan.local), BF16)]
    scratch = [
        pltpu.VMEM((len(blocks) * plan.block, plan.width), BF16),
        pltpu.VMEM((plan.lanes, plan.local), BF16),
        pltpu.VMEM((plan.lanes, plan.local), BF16),
        pltpu.VMEM((plan.lanes, LANES), BF16),
        pltpu.VMEM((plan.lanes, LANES), BF16),
        pltpu.VMEM((plan.local, plan.window), BF16),
    ]
    args = [me, *blocks, *far([output_weight, *masks, *saved])]
    if last:
        in_specs += [layer_of(input_weight.shape[1:], layer)] + [full(w.shape) for w in before]
        args += [*far([input_weight]), *before]
        out_specs += [full(block)] * 4
        out_shape += [jax.ShapeDtypeStruct(block, BF16)] * 4
        scratch += [pltpu.VMEM((plan.total, 3 * plan.local), BF16)]
    area = plan.window * plan.lanes * plan.heads
    return pl.pallas_call(
        functools.partial(attend_back_kernel, plan, slots, len(blocks)),
        grid=(n,),
        in_specs=in_specs,
        out_specs=out_specs,
        out_shape=out_shape,
        scratch_shapes=scratch,
        compiler_params=params(28),
        cost_estimate=cost(6 * n),
        name="attend_back",
    )(*args)


FF_STEPS = 4


def forward_kernel(plan, last, stream, part_a, part_b, part_c, out_bias, gain, shift, up, up_bias, down, down_bias, next_gain, next_shift, middle, lifted, hidden, slope, *rest):
    outs, total = rest[:-1], rest[-1]
    step = pl.program_id(0)

    @pl.when(step == 0)
    def _():
        projected = part_a[...].astype(F32) + part_b[...].astype(F32) + part_c[...].astype(F32)
        values = stream[...] + (projected + out_bias[...])
        middle[...] = values
        center, scale = norm_stats(values)
        lifted[...] = (center * scale * gain[1:2, :] + shift[1:2, :]).astype(BF16)
        total[...] = values + down_bias[...]

    before = dot(lifted[...], up[...]) + up_bias[...]
    cdf = 0.5 + 0.5 * lax.erf(before * (2.0**-0.5))
    density = jnp.exp2(before * before * (-0.5 * LOG2E)) * (2.0 * math.pi) ** -0.5
    act = (before * cdf).astype(BF16)
    hidden[...] = act
    slope[...] = (cdf + before * density).astype(BF16)
    total[...] += dot(act, down[...])

    @pl.when(step == FF_STEPS - 1)
    def _():
        values = total[...]
        if last:
            outs[0][...] = values.astype(BF16)[: plan.rows]
        else:
            outs[0][...] = values
            center, scale = norm_stats(values)
            outs[1][...] = (center * scale * next_gain[0:1, :] + next_shift[0:1, :]).astype(BF16)


def forward_rest(plan, layer, layers, stream, parts, output_bias, gain, shift, up, up_bias, down, down_bias):
    last = layer == layers - 1
    block = (plan.block, plan.width)
    cols = plan.hidden // FF_STEPS
    follow = min(layer + 1, layers - 1)
    wide = pl.BlockSpec((plan.block, cols), lambda j: (0, j))
    row = lambda width: layer_of((1, width), layer)
    if last:
        tail_specs = [full((plan.rows, plan.width))]
        tail = [jax.ShapeDtypeStruct((plan.rows, plan.width), BF16)]
    else:
        tail_specs = [full(block), full(block)]
        tail = [jax.ShapeDtypeStruct(block, F32), jax.ShapeDtypeStruct(block, BF16)]
    return pl.pallas_call(
        functools.partial(forward_kernel, plan, last),
        grid=(FF_STEPS,),
        in_specs=[full(block)] * 4
        + [
            row(plan.width),
            layer_of(gain.shape[1:], layer),
            layer_of(gain.shape[1:], layer),
            pl.BlockSpec((None, plan.width, cols), lambda j: (layer, 0, j)),
            pl.BlockSpec((None, 1, cols), lambda j: (layer, 0, j)),
            pl.BlockSpec((None, cols, plan.width), lambda j: (layer, j, 0)),
            row(plan.width),
            layer_of(gain.shape[1:], follow),
            layer_of(gain.shape[1:], follow),
        ],
        out_specs=[full(block), full(block), wide, wide] + tail_specs,
        out_shape=[
            result(block, F32),
            result(block, BF16),
            result((plan.block, plan.hidden), BF16),
            result((plan.block, plan.hidden), BF16),
        ]
        + tail,
        scratch_shapes=[pltpu.VMEM(block, F32)],
        compiler_params=params(20),
        cost_estimate=cost(5),
        name="forward_rest",
    )(stream, *parts, *far([output_bias, gain, shift]), up, *far([up_bias]), down, *far([down_bias, gain, shift]))


def back_kernel(plan, carry, middle, slope, gain, up, down, low, before_low, middle_grad, middle_low, sums, up_bias, total):
    step = pl.program_id(0)

    @pl.when(step == 0)
    def _():
        low[...] = carry[...].astype(BF16)
        total[...] = jnp.zeros(total.shape, F32)

    before_grad = dot(low[...], down[...], NT) * slope[...].astype(F32)
    up_bias[...] = jnp.sum(before_grad, axis=0, keepdims=True)
    narrow = before_grad.astype(BF16)
    before_low[...] = narrow
    total[...] += dot(narrow, up[...], NT)

    @pl.when(step == FF_STEPS - 1)
    def _():
        center, scale = norm_stats(middle[...])
        grad, gain_sum, shift_sum = norm_back(total[...], center, scale, gain[1:2, :])
        carried = carry[...]
        grad = carried + grad
        middle_grad[...] = grad
        middle_low[...] = grad.astype(BF16)
        sums[...] = jnp.zeros(sums.shape, F32)
        sums[0:1, :] = gain_sum
        sums[1:2, :] = shift_sum
        sums[2:3, :] = jnp.sum(grad, axis=0, keepdims=True)
        sums[3:4, :] = jnp.sum(carried, axis=0, keepdims=True)


def back_rest(plan, layer, carry, middle, slope, gain, up, down, away):
    block = (plan.block, plan.width)
    cols = plan.hidden // FF_STEPS
    wide = pl.BlockSpec((plan.block, cols), lambda j: (0, j))
    return pl.pallas_call(
        functools.partial(back_kernel, plan),
        grid=(FF_STEPS,),
        in_specs=[
            full(block),
            full(block),
            wide,
            layer_of(gain.shape[1:], layer),
            pl.BlockSpec((None, plan.width, cols), lambda j: (layer, 0, j)),
            pl.BlockSpec((None, cols, plan.width), lambda j: (layer, j, 0)),
        ],
        out_specs=[
            full(block),
            wide,
            full(block),
            full(block),
            full((8, plan.width)),
            pl.BlockSpec((1, cols), lambda j: (0, j)),
        ],
        out_shape=[
            jax.ShapeDtypeStruct(block, BF16),
            jax.ShapeDtypeStruct((plan.block, plan.hidden), BF16),
            jax.ShapeDtypeStruct(block, F32),
            jax.ShapeDtypeStruct(block, BF16),
            jax.ShapeDtypeStruct((8, plan.width), F32),
            jax.ShapeDtypeStruct((1, plan.hidden), F32),
        ],
        scratch_shapes=[pltpu.VMEM(block, F32)],
        compiler_params=params(20),
        cost_estimate=cost(6),
        name="back_rest",
    )(carry, *far((middle, slope), away), *far((gain, up, down)))


SMALL_ROWS = 8
CUT = 4


def carry_kernel(plan, wide, me, env_id, part_a, part_b, part_c, stream, middle_grad, gain, *rest):
    others, outs = rest[: len(rest) - 2], rest[-2:]
    carry, sums = outs
    upstream = part_a[...].astype(F32) + part_b[...].astype(F32) + part_c[...].astype(F32)
    center, scale = norm_stats(stream[...])
    grad, gain_sum, shift_sum = norm_back(upstream, center, scale, gain[0:1, :])
    grad = middle_grad[...] + grad
    carry[...] = grad[: carry.shape[0]]
    sums[...] = jnp.zeros(sums.shape, F32)
    sums[0:1, :] = gain_sum
    sums[1:2, :] = shift_sum
    if not others:
        return
    row = lax.broadcasted_iota(jnp.int32, (plan.block, plan.width), 0)
    place = me[0] * plan.rows + row
    envs = sums.shape[0] - SMALL_ROWS * (1 + len(others))
    line = lax.broadcasted_iota(jnp.int32, (envs, plan.width), 0)
    total = jnp.zeros((envs, plan.width), F32)
    for s in range(plan.seqs):
        inside = (row < plan.rows) & (place >= s * plan.length)
        inside = inside & (place < (s + 1) * plan.length)
        part = jnp.sum(jnp.where(inside, grad, 0.0), axis=0, keepdims=True)
        total = total + jnp.where(line == env_id[0:1, s : s + 1], part, 0.0)
    at = SMALL_ROWS
    for ref in others:
        if ref.shape[0] == 1:
            for i in range(SMALL_ROWS):
                sums[at + i : at + i + 1, 0:wide] = ref[:, i * wide : (i + 1) * wide]
        else:
            sums[at : at + SMALL_ROWS, :] = ref[...]
        at += SMALL_ROWS
    sums[at : at + envs, :] = total


def carry_back(plan, layer, me, env_id, envs, parts, stream, middle_grad, gain, others, away):
    block = (plan.block, plan.width)
    first = layer == 0
    rows = plan.rows if first else plan.block
    wide = plan.hidden // SMALL_ROWS
    assert wide <= plan.width and wide % LANES == 0
    small = SMALL_ROWS * (1 + len(others)) + (envs if first else 0)
    return pl.pallas_call(
        functools.partial(carry_kernel, plan, wide),
        grid=(1,),
        in_specs=[pl.BlockSpec(memory_space=SMEM), full(env_id.shape)]
        + [full(block)] * 5
        + [layer_of(gain.shape[1:], layer)]
        + [full(o.shape) for o in others],
        out_specs=[full((rows, plan.width)), full((small, plan.width))],
        out_shape=[
            jax.ShapeDtypeStruct((rows, plan.width), F32),
            jax.ShapeDtypeStruct((small, plan.width), F32),
        ],
        compiler_params=params(16),
        cost_estimate=cost(2),
        name="carry_back",
    )(me, *far([env_id]), *parts, *far([stream], away), middle_grad, *far([gain, *others]))


def emit_small_kernel(plan, layers, envs, small, env, gain, shift, out_bias, up_bias, down_bias):
    wide = plan.hidden // SMALL_ROWS
    at = SMALL_ROWS
    for layer in range(layers):
        second = at
        up = at + SMALL_ROWS
        first = 0 if layer == 0 else at + 2 * SMALL_ROWS
        at += (2 if layer == 0 else 3) * SMALL_ROWS
        gain[layer, 0:1, :] = small[first : first + 1, :]
        shift[layer, 0:1, :] = small[first + 1 : first + 2, :]
        gain[layer, 1:2, :] = small[second : second + 1, :]
        shift[layer, 1:2, :] = small[second + 1 : second + 2, :]
        out_bias[layer : layer + 1, :] = small[second + 2 : second + 3, :]
        down_bias[layer : layer + 1, :] = small[second + 3 : second + 4, :]
        for i in range(SMALL_ROWS):
            up_bias[layer : layer + 1, i * wide : (i + 1) * wide] = small[up + i : up + i + 1, 0:wide]
    env[...] = small[at : at + envs, :]


def emit_small(plan, layers, envs, small):
    shapes = [
        (envs, plan.width),
        (layers, 2, plan.width),
        (layers, 2, plan.width),
        (layers, plan.width),
        (layers, plan.hidden),
        (layers, plan.width),
    ]
    return pl.pallas_call(
        functools.partial(emit_small_kernel, plan, layers, envs),
        grid=(1,),
        in_specs=[full(small.shape)],
        out_specs=[full(s) for s in shapes],
        out_shape=[jax.ShapeDtypeStruct(s, F32) for s in shapes],
        compiler_params=params(8),
        cost_estimate=cost(1),
        name="emit_small",
    )(small)


def feed_grads_kernel(plan, me, lifted, before_low, low, hidden, keep, send, lifted_t, low_t):
    @pl.when(pl.program_id(0) == 0)
    def _():
        lifted_t[...] = lifted[...].T
        low_t[...] = low[...].T

    up = dot(lifted_t[...], before_low[...]).astype(BF16)
    down = dot(low_t[...], hidden[...]).astype(BF16)

    @pl.when(me[0] % 2 == 0)
    def _():
        keep[...] = up
        send[...] = down

    @pl.when(me[0] % 2 == 1)
    def _():
        keep[...] = down
        send[...] = up


def feed_grads(plan, me, lifted, before_low, low, hidden, away):
    block = (plan.block, plan.width)
    cols = plan.hidden // FF_STEPS
    wide = pl.BlockSpec((plan.block, cols), lambda j: (0, j))
    out = pl.BlockSpec((plan.width, cols), lambda j: (0, j))
    shape = result((plan.width, plan.hidden), BF16, True)
    return pl.pallas_call(
        functools.partial(feed_grads_kernel, plan),
        grid=(FF_STEPS,),
        in_specs=[pl.BlockSpec(memory_space=SMEM), full(block), wide, full(block), wide],
        out_specs=[out, out],
        out_shape=[shape, shape],
        scratch_shapes=[pltpu.VMEM((plan.width, plan.block), BF16)] * 2,
        compiler_params=params(16),
        cost_estimate=cost(5),
        name="feed_grads",
    )(me, *far([lifted], away), before_low, low, *far([hidden], away))


def head_grads_kernel(plan, kinds, beside, digit, *refs):
    me, refs = refs[0], refs[1:]
    scratch, refs = refs[-1], refs[:-1]
    columns = []
    for count in kinds:
        blocks, windows, refs = refs[:4], refs[4 : 4 + count], refs[4 + count :]
        place_blocks(plan, me, blocks, scratch)
        rights = [ref[i] for ref in windows for i in range(ref.shape[0])]
        total = None
        for slot, right in enumerate(rights):
            start = pl.multiple_of(plan.sequence(slot, me[0] // 2) * plan.stride, 16)
            part = dot(scratch[pl.ds(start, plan.window), :].T, right)
            total = part if total is None else total + part
        columns.append(total.astype(BF16))
    if beside:
        columns.append(refs[0][...])
        refs = refs[1:]
    value = jnp.concatenate(columns, axis=1) if len(columns) > 1 else columns[0]
    n = len(refs)
    if n == 1:
        refs[0][...] = value
        return
    count = plan.width // n
    for mine in range(n):

        @pl.when(digit[0] == mine)
        def _(mine=mine):
            for j, ref in enumerate(refs):
                at = (mine ^ j) * count
                ref[...] = value[at : at + count]


def head_grads(plan, me, digit, pieces, pairs, beside=()):
    cols = sum(p[1][0].shape[2] for p in pairs) + sum(b.shape[1] for b in beside)
    shape = (plan.width // pieces, cols)
    flat = [a for p in pairs for a in (*p[0], *p[1])] + list(beside)
    return pl.pallas_call(
        functools.partial(head_grads_kernel, plan, [len(p[1]) for p in pairs], len(beside)),
        grid=(1,),
        in_specs=[pl.BlockSpec(memory_space=SMEM)] * 2 + [full(a.shape) for a in flat],
        out_specs=[full(shape)] * pieces,
        out_shape=[jax.ShapeDtypeStruct(shape, BF16)] * pieces,
        scratch_shapes=[pltpu.VMEM((plan.total, plan.width), BF16)],
        compiler_params=params(20),
        cost_estimate=cost(5),
        name="head_grads",
    )(digit, me, *far(flat))


def swap(value, bit):
    size = lax.axis_size("head")
    return lax.ppermute(value, "head", [(i, i ^ bit) for i in range(size)])


def scatter(outs):
    to_diagonal, to_core, to_across, mine = outs
    first = swap(to_diagonal, 1)
    second = swap(to_core, 1)
    pair = (to_across.astype(F32) + first.astype(F32)).astype(BF16)
    return mine, second, swap(pair, 2)


def tie(*trees):
    return lax.optimization_barrier(trees)


class Bits:
    def __init__(self):
        self.heads = lax.axis_size("head")
        self.size = lax.axis_size("seq") * self.heads
        self.place = lax.axis_index("seq") * self.heads + lax.axis_index("head")
        self.place = self.place.astype(jnp.int32)
        seq = [self.heads << i for i in range((self.size // self.heads).bit_length() - 1)]
        self.core, self.across = (1, 1), (2, 2)
        self.seq = [(seq[0], seq[1]), (seq[1], seq[0])] + [(m, m) for m in seq[2:]]

    def bit(self, mask):
        return jnp.where((self.place & mask) > 0, 1, 0).astype(jnp.int32).reshape(1)

    def digit(self, step):
        core = self.place & 1
        value = jnp.int32(0)
        for i, (zero, one) in enumerate(step):
            mask = jnp.where(core == 0, zero, one)
            value = value + jnp.where((self.place & mask) > 0, 1 << i, 0)
        return value.astype(jnp.int32).reshape(1)

    def send(self, value, step, j):
        def partner(place):
            for i, masks in enumerate(step):
                if j >> i & 1:
                    place ^= masks[place & 1]
            return place

        pairs = [(p, partner(p)) for p in range(self.size)]
        return lax.ppermute(value, ("seq", "head"), pairs)


def cut(shape, pieces):
    if shape[0] % (16 * pieces) == 0:
        return 0
    if shape[1] % (LANES * pieces) == 0:
        return 1
    return None


def piece_at(shape, pieces, index):
    dim = cut(shape, pieces) if pieces > 1 else 0
    count = shape[dim] // pieces
    part = tuple(count if d == dim else shape[d] for d in range(2))
    if pieces == 1:
        return (slice(None), slice(None)), part
    window = pl.ds(pl.multiple_of(index * count, 16 if dim == 0 else LANES), count)
    return tuple(window if d == dim else slice(None) for d in range(2)), part


def fold_kernel(pieces, dim, digit, *refs):
    ins, outs = refs[: len(refs) - pieces], refs[len(refs) - pieces :]
    count = ins[0].shape[dim] // pieces
    for j, out in enumerate(outs):
        place = digit[0] ^ j if pieces > 1 else 0
        at = pl.ds(pl.multiple_of(place * count, LANES if dim else 16), count)
        where = (slice(None), at) if dim else (at, slice(None))
        total = ins[0][where].astype(F32)
        for ref in ins[1:]:
            total = total + ref[where].astype(F32)
        out[...] = total.astype(BF16)


def large(shape):
    return shape[0] * shape[1] >= 192 * 1024


def in_columns(shape, dim):
    return 1


def fold(digit, pieces, arrays):
    rows, cols = arrays[0].shape
    dim = cut((rows, cols), pieces)
    part = (rows, cols // pieces) if dim else (rows // pieces, cols)
    steps = in_columns((rows, cols), dim)
    of = lambda shape: pl.BlockSpec((shape[0], shape[1] // steps), lambda j: (0, j))
    return pl.pallas_call(
        functools.partial(fold_kernel, pieces, dim),
        grid=(steps,),
        in_specs=[pl.BlockSpec(memory_space=SMEM)] + [of((rows, cols))] * len(arrays),
        out_specs=[of(part)] * pieces,
        out_shape=[result(part, BF16, large(part))] * pieces,
        compiler_params=params(16),
        cost_estimate=cost(2 if large(arrays[0].shape) else 1),
        name="fold",
    )(digit, *far(arrays, large((rows, cols))))


def join_kernel(dim, digit, own, came, out):
    count = own.shape[dim]
    for j, ref in enumerate((own, came)):
        at = pl.ds(pl.multiple_of((digit[0] ^ j) * count, LANES if dim else 16), count)
        out[(slice(None), at) if dim else (at, slice(None))] = ref[...]


def join(digit, dim, own, came):
    rows, cols = own.shape
    whole = (rows, 2 * cols) if dim else (2 * rows, cols)
    steps = in_columns(whole, dim)
    of = lambda shape: pl.BlockSpec((shape[0], shape[1] // steps), lambda j: (0, j))
    return pl.pallas_call(
        functools.partial(join_kernel, dim),
        grid=(steps,),
        in_specs=[pl.BlockSpec(memory_space=SMEM), of((rows, cols)), of((rows, cols))],
        out_specs=of(whole),
        out_shape=result(whole, BF16, large(whole)),
        compiler_params=params(16),
        cost_estimate=cost(2 if large(whole) else 1),
        name="join",
    )(digit, *far((own, came), large((rows, cols))))


class Chain:
    def __init__(self, bits, plan, keep, send):
        self.bits, self.plan = bits, plan
        self.state = [keep, send]
        self.dims = [None]
        self.at = -1
        self.back = False
        self.done = False

    def work(self):
        bits, plan = self.bits, self.plan
        if not self.back:
            self.at += 1
            if self.at == 0:
                return
            if self.at == len(plan):
                self.at -= 1
                self.back = True
                (own,) = fold(bits.digit([plan[-1]]), 1, self.state)
                self.state = [own, own]
                return
            self.dims.append(cut(self.state[0].shape, 2))
            self.state = list(fold(bits.digit([plan[self.at]]), 2, self.state))
            return
        if self.at == 0:
            self.done = True
            return
        own = join(bits.digit([plan[self.at]]), self.dims[self.at], *self.state)
        self.at -= 1
        self.state = [own, own]

    def going(self):
        return self.state[:1] if self.back and not self.done else self.state

    def exchange(self):
        if not self.done:
            came = self.bits.send(self.state[1], [self.plan[self.at]], 1)
            self.state = [self.state[0], came]


def small_steps(bits):
    return [[b] for b in [bits.core, bits.across] + bits.seq]


def sum_small(bits, step, value):
    came = [bits.send(value, step, j) for j in range(1, 1 << len(step))]
    return functools.reduce(jnp.add, came, value)


def emit_feed_kernel(plan, count, me, digits, *refs):
    sources, (up, down, turned) = refs[: 2 * count], refs[-3:]
    size = plan.width // count
    own, other = sources[:count], sources[count:]
    for core, (ups, downs) in enumerate(((own, other), (other, own))):

        @pl.when(me[0] % 2 == core)
        def _(ups=ups, downs=downs):
            for j in range(count):
                rows = pl.ds(pl.multiple_of((digits[0] ^ j) * size, 16), size)
                up[rows, :] = ups[j][...].astype(F32)
                rows = pl.ds(pl.multiple_of((digits[1] ^ j) * size, 16), size)
                turned[rows, :] = downs[j][...]

    eye = jnp.where(
        lax.broadcasted_iota(jnp.int32, (plan.width, plan.width), 0)
        == lax.broadcasted_iota(jnp.int32, (plan.width, plan.width), 1),
        1.0,
        0.0,
    ).astype(BF16)
    down[...] = dot(turned[...], eye, TN)


def emit_feed(plan, me, digits, layer, layers, sources, before):
    cols = plan.hidden // FF_STEPS
    of = lambda a: pl.BlockSpec((a.shape[0], cols), lambda j: (0, j))
    anywhere = pl.BlockSpec(memory_space=pl.ANY)
    smem = pl.BlockSpec(memory_space=SMEM)

    def kernel(me_ref, digits_ref, *refs):
        ins, outs = refs[: len(sources)], refs[len(sources) + len(before) :]
        emit_feed_kernel(plan, len(sources) // 2, me_ref, digits_ref, *ins, *outs)

    return pl.pallas_call(
        kernel,
        grid=(FF_STEPS,),
        in_specs=[smem, smem] + [of(a) for a in sources] + [anywhere] * len(before),
        out_specs=[
            pl.BlockSpec((None, plan.width, cols), lambda j: (layer, 0, j)),
            pl.BlockSpec((None, cols, plan.width), lambda j: (layer, j, 0)),
        ],
        out_shape=[
            jax.ShapeDtypeStruct((layers, plan.width, plan.hidden), F32),
            jax.ShapeDtypeStruct((layers, plan.hidden, plan.width), F32),
        ],
        scratch_shapes=[pltpu.VMEM((plan.width, cols), BF16)],
        input_output_aliases={2 + len(sources) + i: i for i in range(len(before))},
        compiler_params=params(16),
        cost_estimate=cost(4),
        name="emit_feed",
    )(me, digits, *far(sources), *before)


def emit_heads_kernel(plan, layers, digit, *refs):
    sources, (into, out) = refs[:-2], refs[-2:]
    local = plan.local
    count = plan.width // len(sources)

    def put(ref, rows):
        for layer in range(layers):
            at = layer * 4 * local
            for t in range(3):
                into[layer, t, rows, :] = ref[:, at + t * local : at + (t + 1) * local].astype(F32)
            out[layer, :, rows] = ref[:, at + 3 * local : at + 4 * local].astype(F32).T

    if len(sources) == 1:
        put(sources[0], slice(0, count))
        return
    for mine in range(2):

        @pl.when(digit[0] == mine)
        def _(mine=mine):
            for j, ref in enumerate(sources):
                put(ref, slice((mine ^ j) * count, ((mine ^ j) + 1) * count))


def emit_heads(plan, digit, layers, sources):
    shapes = [(layers, 3, plan.width, plan.local), (layers, plan.local, plan.width)]
    return pl.pallas_call(
        functools.partial(emit_heads_kernel, plan, layers),
        grid=(1,),
        in_specs=[pl.BlockSpec(memory_space=SMEM)] + [full(a.shape) for a in sources],
        out_specs=[full(s) for s in shapes],
        out_shape=[jax.ShapeDtypeStruct(s, F32) for s in shapes],
        compiler_params=params(24),
        cost_estimate=cost(2),
        name="emit_heads",
    )(digit, *far(sources))


def body(
    tokens,
    actions,
    action_mask,
    frame_mask,
    environment_id,
    environment_embed,
    norm_gain,
    norm_bias,
    input_weight,
    output_weight,
    output_bias,
    up_weight,
    up_bias,
    down_weight,
    down_bias,
    cotangent,
):
    rows, width = tokens.shape
    seqs, frames, _ = actions.shape
    layers = input_weight.shape[0]
    envs = environment_embed.shape[0]
    plan = Plan(
        rows,
        lax.axis_size("head"),
        seqs,
        frames,
        width,
        input_weight.shape[3],
        up_weight.shape[2],
    )
    bits = Bits()
    me = lax.axis_index("head").astype(jnp.int32).reshape(1)
    as_rows = lambda t: t.reshape(layers, 1, -1)
    env_row = environment_id.reshape(1, seqs)
    stream, normed, *masks = prologue(
        plan,
        me,
        action_mask,
        frame_mask,
        env_row,
        tokens,
        actions,
        environment_embed,
        norm_gain,
        norm_bias,
    )
    own_slot, other_slots = [0], [1, 2]
    saved = []
    for layer in range(layers):
        away = False
        core, across = swap(normed, 1), swap(normed, 2)
        first = attend(plan, layer, own_slot, me, (normed, core), input_weight, masks, away)
        across, first = tie(across, first)
        blocks = (normed, core, across, swap(across, 1))
        *second, to_diagonal, to_core, to_across, mine = attend(
            plan,
            layer,
            other_slots,
            me,
            blocks,
            input_weight,
            masks,
            away,
            output_weight,
            first[1],
        )
        parts = scatter((to_diagonal, to_core, to_across, mine))
        middle, lifted, hidden, slope, *tail = forward_rest(
            plan,
            layer,
            layers,
            stream,
            parts,
            as_rows(output_bias),
            norm_gain,
            norm_bias,
            up_weight,
            as_rows(up_bias),
            down_weight,
            as_rows(down_bias),
        )
        saved.append((stream, blocks, first, second, middle, lifted, hidden, slope))
        if layer < layers - 1:
            stream, normed = tail
    mixed = tail[0]
    carry = jnp.pad(cotangent.astype(F32), ((0, plan.block - rows), (0, 0)))
    by_steps = len(bits.seq) == 3
    zero = jnp.zeros_like(me)
    stream, blocks, first, second, middle, lifted, hidden, slope = saved[-1]
    last = layers - 1

    def feed_back(layer, carry):
        stream, blocks, first, second, middle, lifted, hidden, slope = saved[layer]
        away = layer < last
        low, before_low, middle_grad, middle_low, second_sums, up_sums = back_rest(
            plan, layer, carry, middle, slope, norm_gain, up_weight, down_weight, away
        )
        core, across = swap(middle_low, 1), swap(middle_low, 2)
        by_chain = by_steps and layer == 0
        if layer == 0:
            own_grad = own_back(layer, middle_low, core)
            lifted, own_grad = tie(lifted, own_grad)
        else:
            lifted, core = tie(lifted, core)
            own_grad = None
        feed = feed_grads(
            plan, me if by_chain else zero, lifted, before_low, low, hidden, away
        )
        core, feed = tie(core, feed)
        return middle_grad, middle_low, core, across, own_grad, feed, second_sums, up_sums

    def own_back(layer, middle_low, core):
        return attend_back(
            plan,
            layer,
            [0],
            me,
            (middle_low, core),
            output_weight,
            masks,
            saved[layer][2],
            True,
        )[0]

    def start(chain, value):
        chain.state, value = tie(chain.state, value)
        chain.work()
        chain.state, value = tie(chain.state, value)
        chain.exchange()
        return value

    feed_plan = [bits.core] + bits.seq[:2] + [bits.across] + bits.seq[2:]
    held = {}

    def finish(state):
        middle_grad, middle_low, core, across, own_grad, last_sums = state
        heads, sums = {}, {}
        feed = None
        for layer in reversed(range(layers)):
            stream, blocks, first, second, middle, lifted, hidden, slope = saved[layer]
            tail = by_steps and layer == 0
            if layer < last:
                middle_grad, middle_low, core, across, own_grad, feed, *last_sums = feed_back(layer, carry)
                if tail:
                    feed = Chain(bits, feed_plan, *feed)
                    across = start(feed, across)
            else:
                across, own_grad = tie(across, own_grad)
            middle_blocks = (middle_low, core, across, swap(across, 1))
            if tail:
                middle_blocks = start(feed, middle_blocks)
            both_grad, *outs = attend_back(
                plan,
                layer,
                [1, 2],
                me,
                middle_blocks,
                output_weight,
                masks,
                second,
                True,
                input_weight,
                (own_grad,),
            )
            if tail:
                outs, feed.state = tie(outs, feed.state)
            to_diagonal, to_core, to_across, mine = outs
            from_diagonal = swap(to_diagonal, 1)
            from_core = swap(to_core, 1)
            pair = (to_across.astype(F32) + from_diagonal.astype(F32)).astype(BF16)
            pair_came = swap(pair, 2)
            if tail:
                feed.work()
                blocks, feed.state = tie(blocks, feed.state)
                feed.exchange()
            out_pair = (middle_blocks, (first[1], second[1]))
            parts = (mine, from_core, pair_came)
            if tail:
                parts, feed.state = tie(parts, feed.state)
            else:
                in_pair = (blocks, (own_grad, both_grad))
                (heads[layer],) = head_grads(plan, me, zero, 1, (in_pair, out_pair))
                parts, heads[layer] = tie(parts, heads[layer])
            carry, sums[layer] = carry_back(
                plan,
                layer,
                me,
                env_row,
                envs,
                parts,
                stream,
                middle_grad,
                norm_gain,
                [] if layer else [*last_sums] + [s for l in range(1, layers) for s in sums[l]],
                True,
            )
            if tail:
                sums[layer] = start(feed, sums[layer])
                blocks, sums[layer] = tie(blocks, sums[layer])
                in_pair = (blocks, (own_grad, both_grad))
                digit = bits.digit([bits.seq[0]])
                halves = head_grads(
                    plan, me, digit, 2, (in_pair, out_pair), [heads[l] for l in range(1, layers)]
                )
                halves, feed.state = tie(halves, feed.state)
                heads = Chain(bits, bits.seq, *halves)
            if layer:
                sums[layer] = (*last_sums, sums[layer])
        small = sums[0]
        if by_steps:
            for step in small_steps(bits)[:CUT]:
                small = start(feed, small)
                small = start(heads, small)
                small = sum_small(bits, step, small)
            for chain in (feed, heads):
                chain.state, small = tie(chain.state, small)
                chain.work()
            held["chains"] = [feed, heads]
            return carry, small, [feed.going(), heads.going()]
        small, feed = lax.psum((small, feed), ("seq", "head"))
        heads = lax.psum(jnp.concatenate([heads[l] for l in range(layers)], axis=1), "seq")
        return carry, small, [list(feed), [heads]]

    assert layers == 2
    middle_grad, middle_low, core, across, _, feed, *last_sums = feed_back(last, carry)
    feed_total = lax.psum(feed, ("seq", "head"))
    own_grad = own_back(last, middle_low, core)
    across, own_grad = tie(across, own_grad)
    state = (middle_grad, middle_low, core, across, own_grad, tuple(last_sums))
    shapes = jax.eval_shape(finish, state)
    carry, small, states = lax.cond(
        frame_mask[0, 0, 0] > 0,
        finish,
        lambda _: jax.tree.map(lambda s: jnp.zeros(s.shape, s.dtype), shapes),
        state,
    )
    states, small, feed_total = tie(states, small, feed_total)
    two = jnp.zeros((2,), jnp.int32)
    if by_steps:
        feed, heads = held["chains"]
        for chain, state in zip((feed, heads), states):
            chain.state = list(state) * (3 - len(state))
        rest = small_steps(bits)[CUT:]
        assert feed.at == 1
        mine = feed.state[0]
        came = bits.send(mine, [feed_plan[1]], 1)
        from_core = bits.send(mine, [bits.core], 1)
        heads.exchange()
        for step in rest:
            small = sum_small(bits, step, small)
        filled = emit_feed(plan, zero, two, last, layers, feed_total, ())
        came, filled, small = tie(came, filled, small)
        also_core = bits.send(came, [bits.core], 1)
        while not heads.done:
            heads.work()
            heads.exchange()
        digits = jnp.concatenate([bits.bit(mask) for mask in feed_plan[1]])
        sources = [mine, came, from_core, also_core]
        feed_out = emit_feed(plan, me, digits, 0, layers, sources, filled)
        digit = bits.digit([bits.seq[0]])
        heads, feed_out = tie(heads.state, feed_out)
    else:
        filled = emit_feed(plan, zero, two, last, layers, feed_total, ())
        feed, heads = states
        feed_out = emit_feed(plan, zero, two, 0, layers, feed, filled)
        digit = zero
    head_out = emit_heads(plan, digit, layers, heads)
    environment_total, gain_out, shift_out, out_bias_out, up_bias_out, down_bias_out = emit_small(
        plan, layers, envs, small
    )
    return (
        mixed,
        carry,
        environment_total,
        gain_out,
        shift_out,
        head_out[0],
        head_out[1],
        out_bias_out,
        feed_out[0],
        up_bias_out,
        feed_out[1],
        down_bias_out,
    )


def solution(mesh):
    return jax.shard_map(
        body,
        mesh=mesh,
        in_specs=(
            P(("seq", "head"), None),
            P("seq", None, None),
            P("seq", None),
            P("seq", None, None),
            P("seq"),
            P(),
            P(),
            P(),
            P(None, None, None, "head"),
            P(None, "head", None),
            P(),
            P(),
            P(),
            P(),
            P(),
            P(("seq", "head"), None),
        ),
        out_specs=(
            P(("seq", "head"), None),
            P(("seq", "head"), None),
            P(),
            P(),
            P(),
            P(None, None, None, "head"),
            P(None, "head", None),
            P(),
            P(),
            P(),
            P(),
            P(),
        ),
        check_vma=False,
    )
```

profile of v0, /device:TPU:0, one launch (start us, length us, event | category | flops | bytes accessed | tf_op | source)
XLA Modules:
  0.0 325.4 jit_solution(5322393033837707883)
XLA Ops:
  7.3 5.4 %prologue.1 = (f32[448,384]{1,0:T(8,128)S(1)}, bf16[448,384]{1,0:T(8,128)(2,1)S(1)}, bf16[3,640,128]{2,1,0:T(8,128)(2,1)S(1)}, bf16[3,640,128]{2,1,0:T(8,128)(2,1)S(1)}, bf16[3,608,128]{2,1,0:T(8,128)(2,1)S(1)}) custom-call(s32[1]{0:T(128)} %bitcast.4.me_ref.refs_0_, s32[3,3]{1,0:T(4,128)} %act_mask.1, s32[3,3,3]{2,1,0:T(4,128)} %frame_mask.1, ...), custom_call_target="tpu_custom_call" | custom-call | bytes 18450000 | tf_op jit(solution)/shard_map/prologue/pallas_call | solution.py:180
  15.8 4.4 %attend.4 = (bf16[1,608,768]{2,1,0:T(8,128)(2,1)}, bf16[1,608,256]{2,1,0:T(8,128)(2,1)S(1)}, f32[1,608,128]{2,1,0:T(8,128)}) custom-call(s32[1]{0:T(128)} %bitcast.4.me_ref.refs_0_, bf16[448,384]{1,0:T(8,128)(2,1)S(1)} %get-tuple-element.372.refs_1_, bf16[448,384]{1,0:T(8,128)(2,1)S(1)} %collective-permute-done.26.refs_2_, bf16[2,3,384,256]{3,2,1,0:T(8,128)(2,1)} %refs_5_.3, ...), custom_call_target="tpu_custom_call" | custom-call | bytes 11070000 | tf_op jit(solution)/shard_map/attend/pallas_call | solution.py:411
  20.2 4.2 %collective-permute-done.27.refs_3_ = bf16[448,384]{1,0:T(8,128)(2,1)S(1)} collective-permute-done((bf16[448,384]{1,0:T(8,128)(2,1)S(1)}, bf16[448,384]{1,0:T(8,128)(2,1)S(1)}, u32[]{:S(2)}, u32[]{:S(2)}) %collective-permute-start.27) | collective-permute-done | bytes 344096 | tf_op jit(solution)/shard_map/ppermute | solution.py:947
  26.2 7.2 %attend.5 = (bf16[2,608,768]{2,1,0:T(8,128)(2,1)}, bf16[2,608,256]{2,1,0:T(8,128)(2,1)}, f32[2,608,128]{2,1,0:T(8,128)}, bf16[448,384]{1,0:T(8,128)(2,1)S(1)}, b...) custom-call(s32[1]{0:T(128)} %bitcast.4.me_ref.refs_0_, ...), custom_call_target="tpu_custom_call" | custom-call | bytes 22140000 | tf_op jit(solution)/shard_map/attend/pallas_call | solution.py:411
  38.9 6.6 %collective-permute-done.31.part_c = bf16[448,384]{1,0:T(8,128)(2,1)S(1)} collective-permute-done((bf16[448,384]{1,0:T(8,128)(2,1)S(1)}, bf16[448,384]{1,0:T(8,128)(2,1)S(1)}, u32[]{:S(2)}, u32[]{:S(2)}) %collective-permute-start.31) | collective-permute-done | bytes 344096 | tf_op jit(solution)/shard_map/ppermute | solution.py:947
  45.4 6.5 %forward_rest.2 = (f32[448,384]{1,0:T(8,128)}, bf16[448,384]{1,0:T(8,128)(2,1)}, bf16[448,2048]{1,0:T(8,128)(2,1)}, bf16[448,2048]{1,0:T(8,128)(2,1)}, f32[448,3...) custom-call(f32[448,384]{1,0:T(8,128)S(1)} %get-tuple-element.371.stream, bf16[448,384]{1,0:T(8,128)(2,1)S(1)} %get-tuple-element.381.part_a, ...), custom_call_target="tpu_custom_call" | custom-call | bytes 18450000 | tf_op jit(solution)/shard_map/forward_rest/pallas_call | solution.py:657
  57.9 4.6 %collective-permute-done.33.refs_3_ = bf16[448,384]{1,0:T(8,128)(2,1)S(1)} collective-permute-done((bf16[448,384]{1,0:T(8,128)(2,1)S(1)}, bf16[448,384]{1,0:T(8,128)(2,1)S(1)}, u32[]{:S(2)}, u32[]{:S(2)}) %collective-permute-start.33) | collective-permute-done | bytes 344096 | tf_op jit(solution)/shard_map/ppermute | solution.py:947
  64.1 7.1 %attend.7 = (bf16[2,608,768]{2,1,0:T(8,128)(2,1)}, bf16[2,608,256]{2,1,0:T(8,128)(2,1)}, f32[2,608,128]{2,1,0:T(8,128)}, bf16[448,384]{1,0:T(8,128)(2,1)S(1)}, b...) custom-call(s32[1]{0:T(128)} %bitcast.4.me_ref.refs_0_, ...), custom_call_target="tpu_custom_call" | custom-call | bytes 22140000 | tf_op jit(solution)/shard_map/attend/pallas_call | solution.py:411
  74.9 8.3 %collective-permute-done.37.part_c = bf16[448,384]{1,0:T(8,128)(2,1)S(1)} collective-permute-done((bf16[448,384]{1,0:T(8,128)(2,1)S(1)}, bf16[448,384]{1,0:T(8,128)(2,1)S(1)}, u32[]{:S(2)}, u32[]{:S(2)}) %collective-permute-start.37) | collective-permute-done | bytes 344096 | tf_op jit(solution)/shard_map/ppermute | solution.py:947
  83.2 6.1 %forward_rest.3 = (f32[448,384]{1,0:T(8,128)S(1)}, bf16[448,384]{1,0:T(8,128)(2,1)S(1)}, bf16[448,2048]{1,0:T(8,128)(2,1)S(1)}, bf16[448,2048]{1,0:T(8,128)(2,1)S(1)}, bf16[441,384]{1,0:T(8,128)(2,1)}) custom-call(f32[448,384]{1,0:T(8,128)S(1)} %get-tuple-element.385.stream, bf16[448,384]{1,0:T(8,128)(2,1)S(1)} %get-tuple-element.392.part_a, ...), custom_call_target="tpu_custom_call" | custom-call | bytes 18450000 | tf_op jit(solution)/shard_map/forward_rest/pallas_call | solution.py:657
  89.3 6.1 %back_rest.3 = (bf16[448,384]{1,0:T(8,128)(2,1)S(1)}, bf16[448,2048]{1,0:T(8,128)(2,1)S(1)}, f32[448,384]{1,0:T(8,128)}, bf16[448,384]{1,0:T(8,128)(2,1)S(1)}, f32[8,384]{1,0:T(8,128)}, /*index=5*/f32[1,2048]{1,0:T(1,128)}) custom-call(f32[448,384]{1,0:T(8,128)S(1)} %pad_convert_fusion.carry, f32[448,384]{1,0:T(8,128)S(1)} %get-tuple-element.397.middle, ...), custom_call_target="tpu_custom_call" | custom-call | bytes 22140000 | tf_op jit(solution)/shard_map/back_rest/pallas_call | solution.py:720
  97.1 4.3 %feed_grads.3 = (bf16[384,2048]{1,0:T(8,128)(2,1)}, bf16[384,2048]{1,0:T(8,128)(2,1)}) custom-call(s32[1]{0:T(128)} %constant.12.clone.1.me.me_ref, bf16[448,384]{1,0:T(8,128)(2,1)S(1)} %get-tuple-element.402.lifted, bf16[448,2048]{1,0:T(8,128)(2,1)S(1)} %get-tuple-element.403.before_low, bf16[448,384]{1,0:T(8,128)(2,1)S(1)} %get-tuple-element.404.low, ...), custom_call_target="tpu_custom_call" | custom-call | bytes 18450000 | tf_op jit(solution)/shard_map/feed_grads/pallas_call | solution.py:883
  105.1 5.7 %attend_back.7 = bf16[1,608,768]{2,1,0:T(8,128)(2,1)S(1)} custom-call(s32[1]{0:T(128)} %bitcast.4.me_ref.refs_0_, bf16[448,384]{1,0:T(8,128)(2,1)S(1)} %get-tuple-element.399.refs_1_, bf16[448,384]{1,0:T(8,128)(2,1)S(1)} %collective-permute-done.39.refs_2_, bf16[2,256,384]{2,1,0:T(8,128)(2,1)} %refs_3_.5, bf16[3,640,128]{2,1,0:T(8,128)(2,1)} %copy-done.22, ...), custom_call_target="tpu_custom_call" | custom-call | bytes 22140000 | tf_op jit(solution)/shard_map/attend_back/pallas_call | solution.py:596
  113.4 164.5 %conditional.1 = (f32[441,384]{1,0:T(8,128)}, f32[56,384]{1,0:T(8,128)}, bf16[192,2048]{1,0:T(8,128)(2,1)}, bf16[96,2048]{1,0:T(8,128)(2,1)}) conditional(s32[]{:T(128)} %bitcast.6, () %tuple.57, (s32[]{:T(128)}, bf16[448,384]{1,0:T(8,128)(2,1)}, bf16[1,608,768]{2,1,0:T(8,128)(2,1)S(1)}, s32[1]{0:T(128)}, bf16[448,384]{1,0:T(8,128)(2,1)S(1)}, ...), branch_computations={%region_0.1_spmd, %region_1.2_spmd} | conditional | flops 1462288 | bytes 381298464 | solution.py:1445
  115.4 13.1 %attend_back.4 = (bf16[2,608,768]{2,1,0:T(8,128)(2,1)S(1)}, bf16[448,384]{1,0:T(8,128)(2,1)S(1)}, bf16[448,384]{1,0:T(8,128)(2,1)S(1)}, bf16[448,384]{1,0:T(8,128)(2,1)S(1)}, bf16[448,384]{1,0:T(8,128)(2,1)S(1)}) custom-call(s32[1]{0:T(128)} %get-tuple-element.84.refs_0_.me, bf16[448,384]{1,0:T(8,128)(2,1)S(1)} %get-tuple-element.87.refs_1_.refs_7_, ...), custom_call_target="tpu_custom_call" | custom-call | bytes 44280000 | tf_op jit(solution)/shard_map/cond/branch_1_fun/attend_back/pallas_call | solution.py:596
  134.3 5.1 %head_grads.2.refs_13_ = bf16[384,1024]{1,0:T(8,128)(2,1)S(1)} custom-call(s32[1]{0:T(128)} %constant.22.clone.digit, s32[1]{0:T(128)} %get-tuple-element.84.refs_0_.me, bf16[448,384]{1,0:T(8,128)(2,1)} %copy-done.29, bf16[448,384]{1,0:T(8,128)(2,1)} %copy-done.30, bf16[448,384]{1,0:T(8,128)(2,1)} %get-tuple-element.107.refs_3_, ...), custom_call_target="tpu_custom_call" | custom-call | bytes 18450000 | tf_op jit(solution)/shard_map/cond/branch_1_fun/head_grads/pallas_call | solution.py:932
  145.4 6.1 %back_rest.2 = (bf16[448,384]{1,0:T(8,128)(2,1)S(1)}, bf16[448,2048]{1,0:T(8,128)(2,1)S(1)}, f32[448,384]{1,0:T(8,128)S(1)}, bf16[448,384]{1,0:T(8,128)(2,1)S(1)...) custom-call(f32[448,384]{1,0:T(8,128)S(1)} %get-tuple-element.117.carry, f32[448,384]{1,0:T(8,128)} %get-tuple-element.118.middle, ...), custom_call_target="tpu_custom_call" | custom-call | bytes 22140000 | tf_op jit(solution)/shard_map/cond/branch_1_fun/back_rest/pallas_call | solution.py:720
  155.2 5.7 %attend_back.5.refs_13_.refs_5_ = bf16[1,608,768]{2,1,0:T(8,128)(2,1)S(1)} custom-call(s32[1]{0:T(128)} %get-tuple-element.84.refs_0_.me, bf16[448,384]{1,0:T(8,128)(2,1)S(1)} %get-tuple-element.147.refs_1_.refs_7_, bf16[448,384]{1,0:T(8,128)(2,1)S(1)} %collective-permute-done.4.refs_2_.refs_8_, bf16[2,256,384]{2,1,0:T(8,128)(2,1)} %get-tuple-element.92.refs_5_.refs_3_, ...), custom_call_target="tpu_custom_call" | custom-call | bytes 22140000 | tf_op jit(solution)/shard_map/cond/branch_1_fun/attend_back/pallas_call | solution.py:596
  160.9 6.0 %feed_grads.2 = (bf16[384,2048]{1,0:T(8,128)(2,1)}, bf16[384,2048]{1,0:T(8,128)(2,1)}) custom-call(s32[1]{0:T(128)} %get-tuple-element.84.refs_0_.me, bf16[448,384]{1,0:T(8,128)(2,1)} %get-tuple-element.127.lifted, bf16[448,2048]{1,0:T(8,128)(2,1)S(1)} %get-tuple-element.128.before_low, bf16[448,384]{1,0:T(8,128)(2,1)S(1)} %get-tuple-element.129.low, ...), custom_call_target="tpu_custom_call" | custom-call | bytes 18450000 | tf_op jit(solution)/shard_map/cond/branch_1_fun/feed_grads/pallas_call | solution.py:883
  175.2 13.5 %attend_back.6 = (bf16[2,608,768]{2,1,0:T(8,128)(2,1)S(1)}, bf16[448,384]{1,0:T(8,128)(2,1)}, bf16[448,384]{1,0:T(8,128)(2,1)S(1)}, bf16[448,384]{1,0:T(8,128)(2,1)S(1)}, bf16[448,384]{1,0:T(8,128)(2,1)S(1)}) custom-call(s32[1]{0:T(128)} %get-tuple-element.84.refs_0_.me, bf16[448,384]{1,0:T(8,128)(2,1)S(1)} %get-tuple-element.147.refs_1_.refs_7_, ...), custom_call_target="tpu_custom_call" | custom-call | bytes 44280000 | tf_op jit(solution)/shard_map/cond/branch_1_fun/attend_back/pallas_call | solution.py:596
  198.9 5.8 %collective-permute-done.12.refs_1_ = bf16[96,2048]{1,0:T(8,128)(2,1)S(1)} collective-permute-done((bf16[96,2048]{1,0:T(8,128)(2,1)}, bf16[96,2048]{1,0:T(8,128)(2,1)S(1)}, u32[]{:S(2)}, u32[]{:S(2)}) %collective-permute-start.12) | collective-permute-done | bytes 393248 | tf_op jit(solution)/shard_map/cond/branch_1_fun/ppermute | solution.py:991
  204.7 3.8 %collective-permute-done.11.part_c = bf16[448,384]{1,0:T(8,128)(2,1)S(1)} collective-permute-done((bf16[448,384]{1,0:T(8,128)(2,1)S(1)}, bf16[448,384]{1,0:T(8,128)(2,1)S(1)}, u32[]{:S(2)}, u32[]{:S(2)}) %collective-permute-start.11) | collective-permute-done | bytes 344096 | tf_op jit(solution)/shard_map/cond/branch_1_fun/ppermute | solution.py:947
  213.3 5.6 %head_grads.3 = (bf16[192,2048]{1,0:T(8,128)(2,1)S(1)}, bf16[192,2048]{1,0:T(8,128)(2,1)S(1)}) custom-call(s32[1]{0:T(128)} %bitcast.digit, s32[1]{0:T(128)} %get-tuple-element.84.refs_0_.me, bf16[448,384]{1,0:T(8,128)(2,1)} %get-tuple-element.199.refs_1_, bf16[448,384]{1,0:T(8,128)(2,1)} %get-tuple-element.200.refs_2_, ...), custom_call_target="tpu_custom_call" | custom-call | bytes 18450000 | tf_op jit(solution)/shard_map/cond/branch_1_fun/head_grads/pallas_call | solution.py:932
  220.3 3.9 %collective-permute-start.15 = (bf16[48,1024]{1,0:T(8,128)(2,1)S(1)}, bf16[48,1024]{1,0:T(8,128)(2,1)S(1)}, u32[]{:S(2)}, u32[]{:S(2)}) collective-permute-start(bf16[48,1024]{1,0:T(8,128)(2,1)S(1)} %get-tuple-element.223), channel_id=1, source_target_pairs={{0,16},{1,17},{2,18},{3,19},{4,20},{5,21},{6,22},{7,23},{8,24},{9,... | collective-permute-start | bytes 294920 | tf_op jit(solution)/shard_map/cond/branch_1_fun/ppermute | solution.py:991
  228.4 6.9 %collective-permute-done.14.refs_1_ = bf16[192,2048]{1,0:T(8,128)(2,1)S(1)} collective-permute-done((bf16[192,2048]{1,0:T(8,128)(2,1)S(1)}, bf16[192,2048]{1,0:T(8,128)(2,1)S(1)}, u32[]{:S(2)}, u32[]{:S(2)}) %collective-permute-start.14) | collective-permute-done | bytes 786464 | tf_op jit(solution)/shard_map/cond/branch_1_fun/ppermute | solution.py:991
  239.6 3.4 %collective-permute-start.18 = (bf16[48,1024]{1,0:T(8,128)(2,1)S(1)}, bf16[48,1024]{1,0:T(8,128)(2,1)S(1)}, u32[]{:S(2)}, u32[]{:S(2)}) collective-permute-start(bf16[48,1024]{1,0:T(8,128)(2,1)S(1)} %fold.12.own), channel_id=1, source_target_pairs={{0,16},{1,17},{2,18},{3,19},{4,20},{5,21},{6,22},{7,23},{8,24},{9,... | collective-permute-start | bytes 294920 | tf_op jit(solution)/shard_map/cond/branch_1_fun/ppermute | solution.py:991
  244.0 3.5 %collective-permute-done.19 = f32[56,384]{1,0:T(8,128)S(1)} collective-permute-done((f32[56,384]{1,0:T(8,128)S(1)}, f32[56,384]{1,0:T(8,128)S(1)}, u32[]{:S(2)}, u32[]{:S(2)}) %collective-permute-start.19) | collective-permute-done | bytes 86048 | tf_op jit(solution)/shard_map/cond/branch_1_fun/ppermute | solution.py:991
  267.0 6.5 %collective-permute-done.25 = f32[56,384]{1,0:T(8,128)S(1)} collective-permute-done((f32[56,384]{1,0:T(8,128)S(1)}, f32[56,384]{1,0:T(8,128)S(1)}, u32[]{:S(2)}, u32[]{:S(2)}) %collective-permute-start.25) | collective-permute-done | bytes 86048 | tf_op jit(solution)/shard_map/cond/branch_1_fun/ppermute | solution.py:991
  285.7 5.3 %emit_feed.2 = (f32[2,384,2048]{2,1,0:T(8,128)}, f32[2,2048,384]{2,1,0:T(8,128)}) custom-call(s32[1]{0:T(128)} %constant.12.clone.1.me.me_ref, s32[2]{0:T(128)S(1)} %broadcast_9_digits_ref.2.digits_ref, bf16[384,2048]{1,0:T(8,128)(2,1)} %get-tuple-element.435.refs_0_, bf16[384,2048]{1,0:T(8,128)(2,1)} %get-tuple-element.436.refs_1_), custom_call_target="tpu_custom_call" | custom-call | bytes 14760000 | tf_op jit(solution)/shard_map/emit_feed/pallas_call | solution.py:1157
  294.2 4.8 %collective-permute-start.45 = (bf16[192,2048]{1,0:T(8,128)(2,1)S(1)}, bf16[192,2048]{1,0:T(8,128)(2,1)S(1)}, u32[]{:S(2)}, u32[]{:S(2)}) collective-permute-start(bf16[192,2048]{1,0:T(8,128)(2,1)S(1)} %collective-permute-done.40.refs_1_), channel_id=1, source_target_pairs={{0,1},{1,0},{2,3},{3,2},{4,5},{5,4},{6,7},{7,6},{8,9},{9,8},{10,11... | collective-permute-start | bytes 2359304 | tf_op jit(solution)/shard_map/ppermute | solution.py:991
  304.9 5.8 %emit_feed.3 = (f32[2,384,2048]{2,1,0:T(8,128)}, f32[2,2048,384]{2,1,0:T(8,128)}) custom-call(s32[1]{0:T(128)} %bitcast.4.me_ref.refs_0_, s32[2]{0:T(128)S(1)} %pad_add_fusion.digits_ref, bf16[192,2048]{1,0:T(8,128)(2,1)} %get-tuple-element.434.refs_0_, bf16[192,2048]{1,0:T(8,128)(2,1)} %copy-done.41, ...), custom_call_target="tpu_custom_call", output_to_operand_aliasing={{0}: (6, {}), {1}: (7, {})} | custom-call | bytes 14760000 | tf_op jit(solution)/shard_map/emit_feed/pallas_call | solution.py:1157
  314.8 3.4 %emit_heads.1 = (f32[2,3,384,256]{3,2,1,0:T(8,128)}, f32[2,256,384]{2,1,0:T(8,128)}) custom-call(s32[1]{0:T(128)} %bitcast.7.digit, bf16[192,2048]{1,0:T(8,128)(2,1)} %join.9.refs_0_, bf16[192,2048]{1,0:T(8,128)(2,1)} %copy-done.44), custom_call_target="tpu_custom_call" | custom-call | bytes 7380000 | tf_op jit(solution)/shard_map/emit_heads/pallas_call | solution.py:1202
  (228 shorter events, 124.9 us)
Async XLA Ops:
  7.2 270.8 %all-reduce.4.cloned.1.call-start = ((), (), s32[]{:S(2)}) async-start(), calls=%async_computation | async-start | bytes 6291456 | tf_op jit(solution)/shard_map/psum | solution.py:1440
  13.2 11.2 %collective-permute-start.27 = (bf16[448,384]{1,0:T(8,128)(2,1)S(1)}, bf16[448,384]{1,0:T(8,128)(2,1)S(1)}, u32[]{:S(2)}, u32[]{:S(2)}) collective-permute-start(bf16[448,384]{1,0:T(8,128)(2,1)S(1)} %get-tuple-element.372.refs_1_), channel_id=1, source_target_pairs={{0,2},{1,3},{2,0},{3,1},{4,6},{5,7},{6,4},{7,5},{8,10},{9,11},{10,... | collective-permute-start | bytes 1032200 | tf_op jit(solution)/shard_map/ppermute | solution.py:947
  33.6 5.2 %collective-permute-start.29 = (bf16[448,384]{1,0:T(8,128)(2,1)S(1)}, bf16[448,384]{1,0:T(8,128)(2,1)S(1)}, u32[]{:S(2)}, u32[]{:S(2)}) collective-permute-start(bf16[448,384]{1,0:T(8,128)(2,1)S(1)} %get-tuple-element.382), channel_id=1, source_target_pairs={{0,1},{1,0},{2,3},{3,2},{4,5},{5,4},{6,7},{7,6},{8,9},{9,8},{10,11... | collective-permute-start | bytes 1032200 | tf_op jit(solution)/shard_map/ppermute | solution.py:947
  35.3 10.2 %collective-permute-start.31 = (bf16[448,384]{1,0:T(8,128)(2,1)S(1)}, bf16[448,384]{1,0:T(8,128)(2,1)S(1)}, u32[]{:S(2)}, u32[]{:S(2)}) collective-permute-start(bf16[448,384]{1,0:T(8,128)(2,1)S(1)} %add_convert_fusion.3), channel_id=1, source_target_pairs={{0,2},{1,3},{2,0},{3,1},{4,6},{5,7},{6,4},{7,5},{8,10},{9,11},{10,... | collective-permute-start | bytes 1032200 | tf_op jit(solution)/shard_map/ppermute | solution.py:947
  52.0 10.5 %collective-permute-start.33 = (bf16[448,384]{1,0:T(8,128)(2,1)S(1)}, bf16[448,384]{1,0:T(8,128)(2,1)S(1)}, u32[]{:S(2)}, u32[]{:S(2)}) collective-permute-start(bf16[448,384]{1,0:T(8,128)(2,1)S(1)} %get-tuple-element.386.refs_1_), channel_id=1, source_target_pairs={{0,2},{1,3},{2,0},{3,1},{4,6},{5,7},{6,4},{7,5},{8,10},{9,11},{10,... | collective-permute-start | bytes 1032200 | tf_op jit(solution)/shard_map/ppermute | solution.py:947
  73.0 10.2 %collective-permute-start.37 = (bf16[448,384]{1,0:T(8,128)(2,1)S(1)}, bf16[448,384]{1,0:T(8,128)(2,1)S(1)}, u32[]{:S(2)}, u32[]{:S(2)}) collective-permute-start(bf16[448,384]{1,0:T(8,128)(2,1)S(1)} %add_convert_fusion.2), channel_id=1, source_target_pairs={{0,2},{1,3},{2,0},{3,1},{4,6},{5,7},{6,4},{7,5},{8,10},{9,11},{10,... | collective-permute-start | bytes 1032200 | tf_op jit(solution)/shard_map/ppermute | solution.py:947
  101.4 12.0 %collective-permute-start.38 = (bf16[448,384]{1,0:T(8,128)(2,1)S(1)}, bf16[448,384]{1,0:T(8,128)(2,1)}, u32[]{:S(2)}, u32[]{:S(2)}) collective-permute-start(bf16[448,384]{1,0:T(8,128)(2,1)S(1)} %get-tuple-element.399.refs_1_), channel_id=1, source_target_pairs={{0,2},{1,3},{2,0},{3,1},{4,6},{5,7},{6,4},{7,5},{8,10},{9,11},{10,... | collective-permute-start | bytes 1032200 | tf_op jit(solution)/shard_map/ppermute | solution.py:947
  130.0 10.3 %collective-permute-start.1 = (bf16[448,384]{1,0:T(8,128)(2,1)S(1)}, bf16[448,384]{1,0:T(8,128)(2,1)S(1)}, u32[]{:S(2)}, u32[]{:S(2)}) collective-permute-start(bf16[448,384]{1,0:T(8,128)(2,1)S(1)} %get-tuple-element.102), channel_id=1, source_target_pairs={{0,1},{1,0},{2,3},{3,2},{4,5},{5,4},{6,7},{7,6},{8,9},{9,8},{10,11... | collective-permute-start | bytes 1032200 | tf_op jit(solution)/shard_map/cond/branch_1_fun/ppermute | solution.py:947
  131.6 12.1 %collective-permute-start.3 = (bf16[448,384]{1,0:T(8,128)(2,1)S(1)}, bf16[448,384]{1,0:T(8,128)(2,1)S(1)}, u32[]{:S(2)}, u32[]{:S(2)}) collective-permute-start(bf16[448,384]{1,0:T(8,128)(2,1)S(1)} %add_convert_fusion.1), channel_id=1, source_target_pairs={{0,2},{1,3},{2,0},{3,1},{4,6},{5,7},{6,4},{7,5},{8,10},{9,11},{10,... | collective-permute-start | bytes 1032200 | tf_op jit(solution)/shard_map/cond/branch_1_fun/ppermute | solution.py:947
  152.7 14.2 %collective-permute-start.5 = (bf16[448,384]{1,0:T(8,128)(2,1)S(1)}, bf16[448,384]{1,0:T(8,128)(2,1)S(1)}, u32[]{:S(2)}, u32[]{:S(2)}) collective-permute-start(bf16[448,384]{1,0:T(8,128)(2,1)S(1)} %get-tuple-element.147.refs_1_.refs_7_), channel_id=1, source_target_pairs={{0,2},{1,3},{2,0},{3,1},{4,6},{5,7},{6,4},{7,5},{8,10},{9,11},{10,... | collective-permute-start | bytes 1032200 | tf_op jit(solution)/shard_map/cond/branch_1_fun/ppermute | solution.py:947
  174.4 17.0 %collective-permute-start.8 = (bf16[192,2048]{1,0:T(8,128)(2,1)}, bf16[192,2048]{1,0:T(8,128)(2,1)S(1)}, u32[]{:S(2)}, u32[]{:S(2)}) collective-permute-start(bf16[192,2048]{1,0:T(8,128)(2,1)} %get-tuple-element.160), channel_id=1, source_target_pairs={{0,4},{1,9},{2,6},{3,11},{4,0},{5,13},{6,2},{7,15},{8,12},{9,1},{1... | collective-permute-start | bytes 2359304 | tf_op jit(solution)/shard_map/cond/branch_1_fun/ppermute | solution.py:991
  192.3 4.6 %collective-permute-start.10 = (bf16[448,384]{1,0:T(8,128)(2,1)}, bf16[448,384]{1,0:T(8,128)(2,1)S(1)}, u32[]{:S(2)}, u32[]{:S(2)}) collective-permute-start(bf16[448,384]{1,0:T(8,128)(2,1)} %get-tuple-element.164), channel_id=1, source_target_pairs={{0,1},{1,0},{2,3},{3,2},{4,5},{5,4},{6,7},{7,6},{8,9},{9,8},{10,11... | collective-permute-start | bytes 1032200 | tf_op jit(solution)/shard_map/cond/branch_1_fun/ppermute | solution.py:947
  192.4 6.5 %collective-permute-start.9 = (bf16[448,384]{1,0:T(8,128)(2,1)}, bf16[448,384]{1,0:T(8,128)(2,1)S(1)}, u32[]{:S(2)}, u32[]{:S(2)}) collective-permute-start(bf16[448,384]{1,0:T(8,128)(2,1)} %copy-done.17), channel_id=1, source_target_pairs={{0,1},{1,0},{2,3},{3,2},{4,5},{5,4},{6,7},{7,6},{8,9},{9,8},{10,11... | collective-permute-start | bytes 1032200 | tf_op jit(solution)/shard_map/cond/branch_1_fun/ppermute | solution.py:947
  195.1 9.6 %collective-permute-start.12 = (bf16[96,2048]{1,0:T(8,128)(2,1)}, bf16[96,2048]{1,0:T(8,128)(2,1)S(1)}, u32[]{:S(2)}, u32[]{:S(2)}) collective-permute-start(bf16[96,2048]{1,0:T(8,128)(2,1)} %get-tuple-element.174), channel_id=1, source_target_pairs={{0,8},{1,5},{2,10},{3,7},{4,12},{5,1},{6,14},{7,3},{8,0},{9,13},{1... | collective-permute-start | bytes 1179656 | tf_op jit(solution)/shard_map/cond/branch_1_fun/ppermute | solution.py:991
  197.0 11.5 %collective-permute-start.11 = (bf16[448,384]{1,0:T(8,128)(2,1)S(1)}, bf16[448,384]{1,0:T(8,128)(2,1)S(1)}, u32[]{:S(2)}, u32[]{:S(2)}) collective-permute-start(bf16[448,384]{1,0:T(8,128)(2,1)S(1)} %add_convert_fusion), channel_id=1, source_target_pairs={{0,2},{1,3},{2,0},{3,1},{4,6},{5,7},{6,4},{7,5},{8,10},{9,11},{10,... | collective-permute-start | bytes 1032200 | tf_op jit(solution)/shard_map/cond/branch_1_fun/ppermute | solution.py:947
  212.5 7.6 %collective-permute-start.13 = (bf16[48,2048]{1,0:T(8,128)(2,1)S(1)}, bf16[48,2048]{1,0:T(8,128)(2,1)S(1)}, u32[]{:S(2)}, u32[]{:S(2)}) collective-permute-start(bf16[48,2048]{1,0:T(8,128)(2,1)S(1)} %get-tuple-element.208), channel_id=1, source_target_pairs={{0,2},{1,3},{2,0},{3,1},{4,6},{5,7},{6,4},{7,5},{8,10},{9,11},{10,... | collective-permute-start | bytes 589832 | tf_op jit(solution)/shard_map/cond/branch_1_fun/ppermute | solution.py:991
  220.2 15.2 %collective-permute-start.14 = (bf16[192,2048]{1,0:T(8,128)(2,1)S(1)}, bf16[192,2048]{1,0:T(8,128)(2,1)S(1)}, u32[]{:S(2)}, u32[]{:S(2)}) collective-permute-start(bf16[192,2048]{1,0:T(8,128)(2,1)S(1)} %get-tuple-element.221), channel_id=1, source_target_pairs={{0,4},{1,9},{2,6},{3,11},{4,0},{5,13},{6,2},{7,15},{8,12},{9,1},{1... | collective-permute-start | bytes 2359304 | tf_op jit(solution)/shard_map/cond/branch_1_fun/ppermute | solution.py:991
  220.3 8.1 %collective-permute-start.15 = (bf16[48,1024]{1,0:T(8,128)(2,1)S(1)}, bf16[48,1024]{1,0:T(8,128)(2,1)S(1)}, u32[]{:S(2)}, u32[]{:S(2)}) collective-permute-start(bf16[48,1024]{1,0:T(8,128)(2,1)S(1)} %get-tuple-element.223), channel_id=1, source_target_pairs={{0,16},{1,17},{2,18},{3,19},{4,20},{5,21},{6,22},{7,23},{8,24},{9,... | collective-permute-start | bytes 294920 | tf_op jit(solution)/shard_map/cond/branch_1_fun/ppermute | solution.py:991
  238.6 11.8 %collective-permute-start.17 = (bf16[96,2048]{1,0:T(8,128)(2,1)}, bf16[96,2048]{1,0:T(8,128)(2,1)S(1)}, u32[]{:S(2)}, u32[]{:S(2)}) collective-permute-start(bf16[96,2048]{1,0:T(8,128)(2,1)} %get-tuple-element.235), channel_id=1, source_target_pairs={{0,8},{1,5},{2,10},{3,7},{4,12},{5,1},{6,14},{7,3},{8,0},{9,13},{1... | collective-permute-start | bytes 1179656 | tf_op jit(solution)/shard_map/cond/branch_1_fun/ppermute | solution.py:991
  239.6 8.9 %collective-permute-start.18 = (bf16[48,1024]{1,0:T(8,128)(2,1)S(1)}, bf16[48,1024]{1,0:T(8,128)(2,1)S(1)}, u32[]{:S(2)}, u32[]{:S(2)}) collective-permute-start(bf16[48,1024]{1,0:T(8,128)(2,1)S(1)} %fold.12.own), channel_id=1, source_target_pairs={{0,16},{1,17},{2,18},{3,19},{4,20},{5,21},{6,22},{7,23},{8,24},{9,... | collective-permute-start | bytes 294920 | tf_op jit(solution)/shard_map/cond/branch_1_fun/ppermute | solution.py:991
  248.4 9.5 %collective-permute-start.21 = (bf16[48,2048]{1,0:T(8,128)(2,1)S(1)}, bf16[48,2048]{1,0:T(8,128)(2,1)S(1)}, u32[]{:S(2)}, u32[]{:S(2)}) collective-permute-start(bf16[48,2048]{1,0:T(8,128)(2,1)S(1)} %join.5.own), channel_id=1, source_target_pairs={{0,2},{1,3},{2,0},{3,1},{4,6},{5,7},{6,4},{7,5},{8,10},{9,11},{10,... | collective-permute-start | bytes 589832 | tf_op jit(solution)/shard_map/cond/branch_1_fun/ppermute | solution.py:991
  252.4 5.5 %collective-permute-start.22 = (f32[56,384]{1,0:T(8,128)S(1)}, f32[56,384]{1,0:T(8,128)S(1)}, u32[]{:S(2)}, u32[]{:S(2)}) collective-permute-start(f32[56,384]{1,0:T(8,128)S(1)} %add.27), channel_id=1, source_target_pairs={{0,4},{1,9},{2,6},{3,11},{4,0},{5,13},{6,2},{7,15},{8,12},{9,1},{1... | collective-permute-start | bytes 258056 | tf_op jit(solution)/shard_map/cond/branch_1_fun/ppermute | solution.py:991
  253.9 8.0 %collective-permute-start.20 = (bf16[48,2048]{1,0:T(8,128)(2,1)S(1)}, bf16[48,2048]{1,0:T(8,128)(2,1)S(1)}, u32[]{:S(2)}, u32[]{:S(2)}) collective-permute-start(bf16[48,2048]{1,0:T(8,128)(2,1)S(1)} %get-tuple-element.249), channel_id=1, source_target_pairs={{0,16},{1,17},{2,18},{3,19},{4,20},{5,21},{6,22},{7,23},{8,24},{9,... | collective-permute-start | bytes 589832 | tf_op jit(solution)/shard_map/cond/branch_1_fun/ppermute | solution.py:991
  258.7 15.4 %collective-permute-start.24 = (bf16[96,2048]{1,0:T(8,128)(2,1)}, bf16[96,2048]{1,0:T(8,128)(2,1)S(1)}, u32[]{:S(2)}, u32[]{:S(2)}) collective-permute-start(bf16[96,2048]{1,0:T(8,128)(2,1)} %join.6.own), channel_id=1, source_target_pairs={{0,8},{1,5},{2,10},{3,7},{4,12},{5,1},{6,14},{7,3},{8,0},{9,13},{1... | collective-permute-start | bytes 1179656 | tf_op jit(solution)/shard_map/cond/branch_1_fun/ppermute | solution.py:991
  262.0 12.8 %collective-permute-start.23 = (bf16[48,2048]{1,0:T(8,128)(2,1)S(1)}, bf16[48,2048]{1,0:T(8,128)(2,1)S(1)}, u32[]{:S(2)}, u32[]{:S(2)}) collective-permute-start(bf16[48,2048]{1,0:T(8,128)(2,1)S(1)} %fold.15.own), channel_id=1, source_target_pairs={{0,16},{1,17},{2,18},{3,19},{4,20},{5,21},{6,22},{7,23},{8,24},{9,... | collective-permute-start | bytes 589832 | tf_op jit(solution)/shard_map/cond/branch_1_fun/ppermute | solution.py:991
  264.0 9.5 %collective-permute-start.25 = (f32[56,384]{1,0:T(8,128)S(1)}, f32[56,384]{1,0:T(8,128)S(1)}, u32[]{:S(2)}, u32[]{:S(2)}) collective-permute-start(f32[56,384]{1,0:T(8,128)S(1)} %add.28), channel_id=1, source_target_pairs={{0,8},{1,5},{2,10},{3,7},{4,12},{5,1},{6,14},{7,3},{8,0},{9,13},{1... | collective-permute-start | bytes 258056 | tf_op jit(solution)/shard_map/cond/branch_1_fun/ppermute | solution.py:991
  278.0 16.2 %collective-permute-start.40 = (bf16[192,2048]{1,0:T(8,128)(2,1)}, bf16[192,2048]{1,0:T(8,128)(2,1)S(1)}, u32[]{:S(2)}, u32[]{:S(2)}) collective-permute-start(bf16[192,2048]{1,0:T(8,128)(2,1)} %get-tuple-element.434.refs_0_), channel_id=1, source_target_pairs={{0,4},{1,9},{2,6},{3,11},{4,0},{5,13},{6,2},{7,15},{8,12},{9,1},{1... | collective-permute-start | bytes 2359304 | tf_op jit(solution)/shard_map/ppermute | solution.py:991
  280.0 18.9 %collective-permute-start.42 = (bf16[96,2048]{1,0:T(8,128)(2,1)}, bf16[96,2048]{1,0:T(8,128)(2,1)S(1)}, u32[]{:S(2)}, u32[]{:S(2)}) collective-permute-start(bf16[96,2048]{1,0:T(8,128)(2,1)} %get-tuple-element.444.own), channel_id=1, source_target_pairs={{0,8},{1,5},{2,10},{3,7},{4,12},{5,1},{6,14},{7,3},{8,0},{9,13},{1... | collective-permute-start | bytes 1179656 | tf_op jit(solution)/shard_map/ppermute | solution.py:991
  281.9 10.9 %collective-permute-start.41 = (f32[56,384]{1,0:T(8,128)}, f32[56,384]{1,0:T(8,128)S(1)}, u32[]{:S(2)}, u32[]{:S(2)}) collective-permute-start(f32[56,384]{1,0:T(8,128)} %get-tuple-element.439), channel_id=1, source_target_pairs={{0,16},{1,17},{2,18},{3,19},{4,20},{5,21},{6,22},{7,23},{8,24},{9,... | collective-permute-start | bytes 258056 | tf_op jit(solution)/shard_map/ppermute | solution.py:991
  282.3 20.7 %collective-permute-start.44 = (bf16[192,2048]{1,0:T(8,128)(2,1)}, bf16[192,2048]{1,0:T(8,128)(2,1)S(1)}, u32[]{:S(2)}, u32[]{:S(2)}) collective-permute-start(bf16[192,2048]{1,0:T(8,128)(2,1)} %get-tuple-element.434.refs_0_), channel_id=1, source_target_pairs={{0,1},{1,0},{2,3},{3,2},{4,5},{5,4},{6,7},{7,6},{8,9},{9,8},{10,11... | collective-permute-start | bytes 2359304 | tf_op jit(solution)/shard_map/ppermute | solution.py:991
  294.2 8.9 %collective-permute-start.45 = (bf16[192,2048]{1,0:T(8,128)(2,1)S(1)}, bf16[192,2048]{1,0:T(8,128)(2,1)S(1)}, u32[]{:S(2)}, u32[]{:S(2)}) collective-permute-start(bf16[192,2048]{1,0:T(8,128)(2,1)S(1)} %collective-permute-done.40.refs_1_), channel_id=1, source_target_pairs={{0,1},{1,0},{2,3},{3,2},{4,5},{5,4},{6,7},{7,6},{8,9},{9,8},{10,11... | collective-permute-start | bytes 2359304 | tf_op jit(solution)/shard_map/ppermute | solution.py:991
  301.8 12.2 %collective-permute-start.43 = (bf16[192,2048]{1,0:T(8,128)(2,1)}, bf16[192,2048]{1,0:T(8,128)(2,1)S(1)}, u32[]{:S(2)}, u32[]{:S(2)}) collective-permute-start(bf16[192,2048]{1,0:T(8,128)(2,1)} %join.9.refs_0_), channel_id=1, source_target_pairs={{0,4},{1,9},{2,6},{3,11},{4,0},{5,13},{6,2},{7,15},{8,12},{9,1},{1... | collective-permute-start | bytes 2359304 | tf_op jit(solution)/shard_map/ppermute | solution.py:991
  (71 other events, 741.9 us)
Sparse Core Ops, SparseCore 0:
  101.5 146.7 all-reduce.3
where the time goes:
time: 332 us; the launch traced here: 325 us
  Pallas kernels  146 us (44%)
  waiting for transfers between devices  83.8 us (25%)
  starting transfers between devices  60.8 us (18%)
  local copies, waits for them, and re-layouts  16.8 us (5%)
  between operations  15.2 us (5%)
    ppermute x24, waiting for transfers between devices, swap(): return lax.ppermute(value, 'head', [(i, i ^ bit) for i in range(size)])  47.2 us
    ppermute x22, starting transfers between devices, send(): return lax.ppermute(value, ('seq', 'head'), pairs)  40.7 us
    pallas_call x4, Pallas kernels, attend_back(): pl.pallas_call(functools.partial(attend_back_kernel, plan, slots, len(blo...  37.9 us
    ppermute x22, waiting for transfers between devices, send(): return lax.ppermute(value, ('seq', 'head'), pairs)  36.5 us
    pallas_call x4, Pallas kernels, attend(): pl.pallas_call(functools.partial(attend_kernel, plan, slots, len(blocks))...  21.1 us
    ppermute x24, starting transfers between devices, swap(): return lax.ppermute(value, 'head', [(i, i ^ bit) for i in range(size)])  20 us
    pallas_call x2, Pallas kernels, forward_rest(): pl.pallas_call(functools.partial(forward_kernel, plan, last), grid=(FF_ST...  12.6 us
    pallas_call x2, Pallas kernels, back_rest(): pl.pallas_call(functools.partial(back_kernel, plan), grid=(FF_STEPS,), in...  12.2 us
  transfers between devices with their start and end apart: 47, of which 30 were waited for; matrix products, arithmetic and copies ran while one was open for 2% of the time, Pallas kernels for 31%

commit v1 on v0

--- a/solution.py
+++ b/solution.py
@@ -606,7 +606,7 @@
     )(*args)
 
 
-FF_STEPS = 4
+FF_STEPS = 2
 
 
 def forward_kernel(plan, last, stream, part_a, part_b, part_c, out_bias, gain, shift, up, up_bias, down, down_bias, next_gain, next_shift, middle, lifted, hidden, slope, *rest):

time: 332 us -> 330 us (level)
  Pallas kernels: 146 us -> 141 us
  transfers between devices with their start and end apart: 47 -> 47, of which waited for: 30 -> 27; matrix products, arithmetic and copies ran while one was open for 2% -> 2% of each run, Pallas kernels for 31% -> 30%
where the time goes in v1:
time: 330 us; the launch traced here: 324 us
  Pallas kernels  141 us (43%)
  waiting for transfers between devices  86.9 us (26%)
  starting transfers between devices  61.2 us (19%)
  local copies, waits for them, and re-layouts  16.8 us (5%)
  between operations  15.5 us (5%)
    ppermute x24, waiting for transfers between devices, swap(): return lax.ppermute(value, 'head', [(i, i ^ bit) for i in range(size)])  47.9 us
    ppermute x22, starting transfers between devices, send(): return lax.ppermute(value, ('seq', 'head'), pairs)  41.1 us
    ppermute x22, waiting for transfers between devices, send(): return lax.ppermute(value, ('seq', 'head'), pairs)  38.9 us
    pallas_call x4, Pallas kernels, attend_back(): pl.pallas_call(functools.partial(attend_back_kernel, plan, slots, len(blo...  37.7 us
    pallas_call x4, Pallas kernels, attend(): pl.pallas_call(functools.partial(attend_kernel, plan, slots, len(blocks))...  21.2 us
    ppermute x24, starting transfers between devices, swap(): return lax.ppermute(value, 'head', [(i, i ^ bit) for i in range(size)])  20 us
    pallas_call x2, Pallas kernels, forward_rest(): pl.pallas_call(functools.partial(forward_kernel, plan, last), grid=(FF_ST...  11.9 us
    pallas_call x2, Pallas kernels, back_rest(): pl.pallas_call(functools.partial(back_kernel, plan), grid=(FF_STEPS,), in...  11 us
  transfers between devices with their start and end apart: 47, of which 27 were waited for; matrix products, arithmetic and copies ran while one was open for 2% of the time, Pallas kernels for 30%

profile of v1, /device:TPU:0, one launch (start us, length us, event | category | flops | bytes accessed | tf_op | source)
XLA Modules:
  0.0 323.7 jit_solution(508984832268843000)
XLA Ops:
  7.3 5.4 %prologue.1 = (f32[448,384]{1,0:T(8,128)S(1)}, bf16[448,384]{1,0:T(8,128)(2,1)S(1)}, bf16[3,640,128]{2,1,0:T(8,128)(2,1)S(1)}, bf16[3,640,128]{2,1,0:T(8,128)(2,1)S(1)}, bf16[3,608,128]{2,1,0:T(8,128)(2,1)S(1)}) custom-call(s32[1]{0:T(128)} %bitcast.4.me_ref.refs_0_, s32[3,3]{1,0:T(4,128)} %act_mask.1, s32[3,3,3]{2,1,0:T(4,128)} %frame_mask.1, ...), custom_call_target="tpu_custom_call" | custom-call | bytes 18450000 | tf_op jit(solution)/shard_map/prologue/pallas_call | solution.py:180
  15.8 4.4 %attend.4 = (bf16[1,608,768]{2,1,0:T(8,128)(2,1)}, bf16[1,608,256]{2,1,0:T(8,128)(2,1)S(1)}, f32[1,608,128]{2,1,0:T(8,128)}) custom-call(s32[1]{0:T(128)} %bitcast.4.me_ref.refs_0_, bf16[448,384]{1,0:T(8,128)(2,1)S(1)} %get-tuple-element.372.refs_1_, bf16[448,384]{1,0:T(8,128)(2,1)S(1)} %collective-permute-done.26.refs_2_, bf16[2,3,384,256]{3,2,1,0:T(8,128)(2,1)} %refs_5_.3, ...), custom_call_target="tpu_custom_call" | custom-call | bytes 11070000 | tf_op jit(solution)/shard_map/attend/pallas_call | solution.py:411
  20.2 4.2 %collective-permute-done.27.refs_3_ = bf16[448,384]{1,0:T(8,128)(2,1)S(1)} collective-permute-done((bf16[448,384]{1,0:T(8,128)(2,1)S(1)}, bf16[448,384]{1,0:T(8,128)(2,1)S(1)}, u32[]{:S(2)}, u32[]{:S(2)}) %collective-permute-start.27) | collective-permute-done | bytes 344096 | tf_op jit(solution)/shard_map/ppermute | solution.py:947
  26.2 7.3 %attend.5 = (bf16[2,608,768]{2,1,0:T(8,128)(2,1)}, bf16[2,608,256]{2,1,0:T(8,128)(2,1)}, f32[2,608,128]{2,1,0:T(8,128)}, bf16[448,384]{1,0:T(8,128)(2,1)S(1)}, b...) custom-call(s32[1]{0:T(128)} %bitcast.4.me_ref.refs_0_, ...), custom_call_target="tpu_custom_call" | custom-call | bytes 22140000 | tf_op jit(solution)/shard_map/attend/pallas_call | solution.py:411
  38.9 6.6 %collective-permute-done.31.part_c = bf16[448,384]{1,0:T(8,128)(2,1)S(1)} collective-permute-done((bf16[448,384]{1,0:T(8,128)(2,1)S(1)}, bf16[448,384]{1,0:T(8,128)(2,1)S(1)}, u32[]{:S(2)}, u32[]{:S(2)}) %collective-permute-start.31) | collective-permute-done | bytes 344096 | tf_op jit(solution)/shard_map/ppermute | solution.py:947
  45.5 6.2 %forward_rest.2 = (f32[448,384]{1,0:T(8,128)}, bf16[448,384]{1,0:T(8,128)(2,1)}, bf16[448,2048]{1,0:T(8,128)(2,1)}, bf16[448,2048]{1,0:T(8,128)(2,1)}, f32[448,3...) custom-call(f32[448,384]{1,0:T(8,128)S(1)} %get-tuple-element.371.stream, bf16[448,384]{1,0:T(8,128)(2,1)S(1)} %get-tuple-element.381.part_a, ...), custom_call_target="tpu_custom_call" | custom-call | bytes 18450000 | tf_op jit(solution)/shard_map/forward_rest/pallas_call | solution.py:657
  57.6 4.6 %collective-permute-done.33.refs_3_ = bf16[448,384]{1,0:T(8,128)(2,1)S(1)} collective-permute-done((bf16[448,384]{1,0:T(8,128)(2,1)S(1)}, bf16[448,384]{1,0:T(8,128)(2,1)S(1)}, u32[]{:S(2)}, u32[]{:S(2)}) %collective-permute-start.33) | collective-permute-done | bytes 344096 | tf_op jit(solution)/shard_map/ppermute | solution.py:947
  63.9 7.1 %attend.7 = (bf16[2,608,768]{2,1,0:T(8,128)(2,1)}, bf16[2,608,256]{2,1,0:T(8,128)(2,1)}, f32[2,608,128]{2,1,0:T(8,128)}, bf16[448,384]{1,0:T(8,128)(2,1)S(1)}, b...) custom-call(s32[1]{0:T(128)} %bitcast.4.me_ref.refs_0_, ...), custom_call_target="tpu_custom_call" | custom-call | bytes 22140000 | tf_op jit(solution)/shard_map/attend/pallas_call | solution.py:411
  74.6 8.3 %collective-permute-done.37.part_c = bf16[448,384]{1,0:T(8,128)(2,1)S(1)} collective-permute-done((bf16[448,384]{1,0:T(8,128)(2,1)S(1)}, bf16[448,384]{1,0:T(8,128)(2,1)S(1)}, u32[]{:S(2)}, u32[]{:S(2)}) %collective-permute-start.37) | collective-permute-done | bytes 344096 | tf_op jit(solution)/shard_map/ppermute | solution.py:947
  82.9 5.7 %forward_rest.3 = (f32[448,384]{1,0:T(8,128)S(1)}, bf16[448,384]{1,0:T(8,128)(2,1)S(1)}, bf16[448,2048]{1,0:T(8,128)(2,1)S(1)}, bf16[448,2048]{1,0:T(8,128)(2,1)S(1)}, bf16[441,384]{1,0:T(8,128)(2,1)}) custom-call(f32[448,384]{1,0:T(8,128)S(1)} %get-tuple-element.385.stream, bf16[448,384]{1,0:T(8,128)(2,1)S(1)} %get-tuple-element.392.part_a, ...), custom_call_target="tpu_custom_call" | custom-call | bytes 18450000 | tf_op jit(solution)/shard_map/forward_rest/pallas_call | solution.py:657
  88.6 5.5 %back_rest.3 = (bf16[448,384]{1,0:T(8,128)(2,1)S(1)}, bf16[448,2048]{1,0:T(8,128)(2,1)S(1)}, f32[448,384]{1,0:T(8,128)}, bf16[448,384]{1,0:T(8,128)(2,1)S(1)}, f32[8,384]{1,0:T(8,128)}, /*index=5*/f32[1,2048]{1,0:T(1,128)}) custom-call(f32[448,384]{1,0:T(8,128)S(1)} %pad_convert_fusion.carry, f32[448,384]{1,0:T(8,128)S(1)} %get-tuple-element.397.middle, ...), custom_call_target="tpu_custom_call" | custom-call | bytes 22140000 | tf_op jit(solution)/shard_map/back_rest/pallas_call | solution.py:720
  95.7 4.0 %feed_grads.3 = (bf16[384,2048]{1,0:T(8,128)(2,1)}, bf16[384,2048]{1,0:T(8,128)(2,1)}) custom-call(s32[1]{0:T(128)} %constant.12.clone.1.me.me_ref, bf16[448,384]{1,0:T(8,128)(2,1)S(1)} %get-tuple-element.402.lifted, bf16[448,2048]{1,0:T(8,128)(2,1)S(1)} %get-tuple-element.403.before_low, bf16[448,384]{1,0:T(8,128)(2,1)S(1)} %get-tuple-element.404.low, ...), custom_call_target="tpu_custom_call" | custom-call | bytes 18450000 | tf_op jit(solution)/shard_map/feed_grads/pallas_call | solution.py:883
  103.4 5.6 %attend_back.7 = bf16[1,608,768]{2,1,0:T(8,128)(2,1)S(1)} custom-call(s32[1]{0:T(128)} %bitcast.4.me_ref.refs_0_, bf16[448,384]{1,0:T(8,128)(2,1)S(1)} %get-tuple-element.399.refs_1_, bf16[448,384]{1,0:T(8,128)(2,1)S(1)} %collective-permute-done.39.refs_2_, bf16[2,256,384]{2,1,0:T(8,128)(2,1)} %refs_3_.5, bf16[3,640,128]{2,1,0:T(8,128)(2,1)} %copy-done.22, ...), custom_call_target="tpu_custom_call" | custom-call | bytes 22140000 | tf_op jit(solution)/shard_map/attend_back/pallas_call | solution.py:596
  111.8 164.0 %conditional.1 = (f32[441,384]{1,0:T(8,128)}, f32[56,384]{1,0:T(8,128)}, bf16[192,2048]{1,0:T(8,128)(2,1)}, bf16[96,2048]{1,0:T(8,128)(2,1)}) conditional(s32[]{:T(128)} %bitcast.6, () %tuple.57, (s32[]{:T(128)}, bf16[448,384]{1,0:T(8,128)(2,1)}, bf16[1,608,768]{2,1,0:T(8,128)(2,1)S(1)}, s32[1]{0:T(128)}, bf16[448,384]{1,0:T(8,128)(2,1)S(1)}, ...), branch_computations={%region_0.1_spmd, %region_1.2_spmd} | conditional | flops 1462288 | bytes 381298464 | solution.py:1445
  113.8 12.8 %attend_back.4 = (bf16[2,608,768]{2,1,0:T(8,128)(2,1)S(1)}, bf16[448,384]{1,0:T(8,128)(2,1)S(1)}, bf16[448,384]{1,0:T(8,128)(2,1)S(1)}, bf16[448,384]{1,0:T(8,128)(2,1)S(1)}, bf16[448,384]{1,0:T(8,128)(2,1)S(1)}) custom-call(s32[1]{0:T(128)} %get-tuple-element.84.refs_0_.me, bf16[448,384]{1,0:T(8,128)(2,1)S(1)} %get-tuple-element.87.refs_1_.refs_7_, ...), custom_call_target="tpu_custom_call" | custom-call | bytes 44280000 | tf_op jit(solution)/shard_map/cond/branch_1_fun/attend_back/pallas_call | solution.py:596
  132.4 5.1 %head_grads.2.refs_13_ = bf16[384,1024]{1,0:T(8,128)(2,1)S(1)} custom-call(s32[1]{0:T(128)} %constant.22.clone.digit, s32[1]{0:T(128)} %get-tuple-element.84.refs_0_.me, bf16[448,384]{1,0:T(8,128)(2,1)} %copy-done.29, bf16[448,384]{1,0:T(8,128)(2,1)} %copy-done.30, bf16[448,384]{1,0:T(8,128)(2,1)} %get-tuple-element.107.refs_3_, ...), custom_call_target="tpu_custom_call" | custom-call | bytes 18450000 | tf_op jit(solution)/shard_map/cond/branch_1_fun/head_grads/pallas_call | solution.py:932
  143.3 5.5 %back_rest.2 = (bf16[448,384]{1,0:T(8,128)(2,1)S(1)}, bf16[448,2048]{1,0:T(8,128)(2,1)S(1)}, f32[448,384]{1,0:T(8,128)S(1)}, bf16[448,384]{1,0:T(8,128)(2,1)S(1)...) custom-call(f32[448,384]{1,0:T(8,128)S(1)} %get-tuple-element.117.carry, f32[448,384]{1,0:T(8,128)} %get-tuple-element.118.middle, ...), custom_call_target="tpu_custom_call" | custom-call | bytes 22140000 | tf_op jit(solution)/shard_map/cond/branch_1_fun/back_rest/pallas_call | solution.py:720
  152.6 5.7 %attend_back.5.refs_13_.refs_5_ = bf16[1,608,768]{2,1,0:T(8,128)(2,1)S(1)} custom-call(s32[1]{0:T(128)} %get-tuple-element.84.refs_0_.me, bf16[448,384]{1,0:T(8,128)(2,1)S(1)} %get-tuple-element.147.refs_1_.refs_7_, bf16[448,384]{1,0:T(8,128)(2,1)S(1)} %collective-permute-done.4.refs_2_.refs_8_, bf16[2,256,384]{2,1,0:T(8,128)(2,1)} %get-tuple-element.92.refs_5_.refs_3_, ...), custom_call_target="tpu_custom_call" | custom-call | bytes 22140000 | tf_op jit(solution)/shard_map/cond/branch_1_fun/attend_back/pallas_call | solution.py:596
  158.3 5.4 %feed_grads.2 = (bf16[384,2048]{1,0:T(8,128)(2,1)}, bf16[384,2048]{1,0:T(8,128)(2,1)}) custom-call(s32[1]{0:T(128)} %get-tuple-element.84.refs_0_.me, bf16[448,384]{1,0:T(8,128)(2,1)} %get-tuple-element.127.lifted, bf16[448,2048]{1,0:T(8,128)(2,1)S(1)} %get-tuple-element.128.before_low, bf16[448,384]{1,0:T(8,128)(2,1)S(1)} %get-tuple-element.129.low, ...), custom_call_target="tpu_custom_call" | custom-call | bytes 18450000 | tf_op jit(solution)/shard_map/cond/branch_1_fun/feed_grads/pallas_call | solution.py:883
  171.6 13.5 %attend_back.6 = (bf16[2,608,768]{2,1,0:T(8,128)(2,1)S(1)}, bf16[448,384]{1,0:T(8,128)(2,1)}, bf16[448,384]{1,0:T(8,128)(2,1)S(1)}, bf16[448,384]{1,0:T(8,128)(2,1)S(1)}, bf16[448,384]{1,0:T(8,128)(2,1)S(1)}) custom-call(s32[1]{0:T(128)} %get-tuple-element.84.refs_0_.me, bf16[448,384]{1,0:T(8,128)(2,1)S(1)} %get-tuple-element.147.refs_1_.refs_7_, ...), custom_call_target="tpu_custom_call" | custom-call | bytes 44280000 | tf_op jit(solution)/shard_map/cond/branch_1_fun/attend_back/pallas_call | solution.py:596
  195.5 5.2 %collective-permute-done.12.refs_1_ = bf16[96,2048]{1,0:T(8,128)(2,1)S(1)} collective-permute-done((bf16[96,2048]{1,0:T(8,128)(2,1)}, bf16[96,2048]{1,0:T(8,128)(2,1)S(1)}, u32[]{:S(2)}, u32[]{:S(2)}) %collective-permute-start.12) | collective-permute-done | bytes 393248 | tf_op jit(solution)/shard_map/cond/branch_1_fun/ppermute | solution.py:991
  200.7 4.7 %collective-permute-done.11.part_c = bf16[448,384]{1,0:T(8,128)(2,1)S(1)} collective-permute-done((bf16[448,384]{1,0:T(8,128)(2,1)S(1)}, bf16[448,384]{1,0:T(8,128)(2,1)S(1)}, u32[]{:S(2)}, u32[]{:S(2)}) %collective-permute-start.11) | collective-permute-done | bytes 344096 | tf_op jit(solution)/shard_map/cond/branch_1_fun/ppermute | solution.py:947
  210.7 5.5 %head_grads.3 = (bf16[192,2048]{1,0:T(8,128)(2,1)S(1)}, bf16[192,2048]{1,0:T(8,128)(2,1)S(1)}) custom-call(s32[1]{0:T(128)} %bitcast.digit, s32[1]{0:T(128)} %get-tuple-element.84.refs_0_.me, bf16[448,384]{1,0:T(8,128)(2,1)} %get-tuple-element.199.refs_1_, bf16[448,384]{1,0:T(8,128)(2,1)} %get-tuple-element.200.refs_2_, ...), custom_call_target="tpu_custom_call" | custom-call | bytes 18450000 | tf_op jit(solution)/shard_map/cond/branch_1_fun/head_grads/pallas_call | solution.py:932
  222.0 4.2 %collective-permute-done.15.refs_1_ = bf16[48,1024]{1,0:T(8,128)(2,1)S(1)} collective-permute-done((bf16[48,1024]{1,0:T(8,128)(2,1)S(1)}, bf16[48,1024]{1,0:T(8,128)(2,1)S(1)}, u32[]{:S(2)}, u32[]{:S(2)}) %collective-permute-start.15) | collective-permute-done | bytes 98336 | tf_op jit(solution)/shard_map/cond/branch_1_fun/ppermute | solution.py:991
  226.2 6.5 %collective-permute-done.14.refs_1_ = bf16[192,2048]{1,0:T(8,128)(2,1)S(1)} collective-permute-done((bf16[192,2048]{1,0:T(8,128)(2,1)S(1)}, bf16[192,2048]{1,0:T(8,128)(2,1)S(1)}, u32[]{:S(2)}, u32[]{:S(2)}) %collective-permute-start.14) | collective-permute-done | bytes 786464 | tf_op jit(solution)/shard_map/cond/branch_1_fun/ppermute | solution.py:991
  256.5 3.7 %collective-permute-start.24 = (bf16[96,2048]{1,0:T(8,128)(2,1)}, bf16[96,2048]{1,0:T(8,128)(2,1)S(1)}, u32[]{:S(2)}, u32[]{:S(2)}) collective-permute-start(bf16[96,2048]{1,0:T(8,128)(2,1)} %join.6.own), channel_id=1, source_target_pairs={{0,8},{1,5},{2,10},{3,7},{4,12},{5,1},{6,14},{7,3},{8,0},{9,13},{1... | collective-permute-start | bytes 1179656 | tf_op jit(solution)/shard_map/cond/branch_1_fun/ppermute | solution.py:991
  264.6 6.7 %collective-permute-done.25 = f32[56,384]{1,0:T(8,128)S(1)} collective-permute-done((f32[56,384]{1,0:T(8,128)S(1)}, f32[56,384]{1,0:T(8,128)S(1)}, u32[]{:S(2)}, u32[]{:S(2)}) %collective-permute-start.25) | collective-permute-done | bytes 86048 | tf_op jit(solution)/shard_map/cond/branch_1_fun/ppermute | solution.py:991
  280.2 3.9 %collective-permute-start.44 = (bf16[192,2048]{1,0:T(8,128)(2,1)}, bf16[192,2048]{1,0:T(8,128)(2,1)S(1)}, u32[]{:S(2)}, u32[]{:S(2)}) collective-permute-start(bf16[192,2048]{1,0:T(8,128)(2,1)} %get-tuple-element.434.refs_0_), channel_id=1, source_target_pairs={{0,1},{1,0},{2,3},{3,2},{4,5},{5,4},{6,7},{7,6},{8,9},{9,8},{10,11... | collective-permute-start | bytes 2359304 | tf_op jit(solution)/shard_map/ppermute | solution.py:991
  284.1 4.3 %emit_feed.2 = (f32[2,384,2048]{2,1,0:T(8,128)}, f32[2,2048,384]{2,1,0:T(8,128)}) custom-call(s32[1]{0:T(128)} %constant.12.clone.1.me.me_ref, s32[2]{0:T(128)S(1)} %broadcast_9_digits_ref.2.digits_ref, bf16[384,2048]{1,0:T(8,128)(2,1)} %get-tuple-element.435.refs_0_, bf16[384,2048]{1,0:T(8,128)(2,1)} %get-tuple-element.436.refs_1_), custom_call_target="tpu_custom_call" | custom-call | bytes 14760000 | tf_op jit(solution)/shard_map/emit_feed/pallas_call | solution.py:1157
  292.3 4.7 %collective-permute-start.45 = (bf16[192,2048]{1,0:T(8,128)(2,1)S(1)}, bf16[192,2048]{1,0:T(8,128)(2,1)S(1)}, u32[]{:S(2)}, u32[]{:S(2)}) collective-permute-start(bf16[192,2048]{1,0:T(8,128)(2,1)S(1)} %collective-permute-done.40.refs_1_), channel_id=1, source_target_pairs={{0,1},{1,0},{2,3},{3,2},{4,5},{5,4},{6,7},{7,6},{8,9},{9,8},{10,11... | collective-permute-start | bytes 2359304 | tf_op jit(solution)/shard_map/ppermute | solution.py:991
  302.7 4.3 %emit_feed.3 = (f32[2,384,2048]{2,1,0:T(8,128)}, f32[2,2048,384]{2,1,0:T(8,128)}) custom-call(s32[1]{0:T(128)} %bitcast.4.me_ref.refs_0_, s32[2]{0:T(128)S(1)} %pad_add_fusion.digits_ref, bf16[192,2048]{1,0:T(8,128)(2,1)} %get-tuple-element.434.refs_0_, bf16[192,2048]{1,0:T(8,128)(2,1)} %copy-done.41, ...), custom_call_target="tpu_custom_call", output_to_operand_aliasing={{0}: (6, {}), {1}: (7, {})} | custom-call | bytes 14760000 | tf_op jit(solution)/shard_map/emit_feed/pallas_call | solution.py:1157
  307.1 4.9 %collective-permute-done.43.refs_1_ = bf16[192,2048]{1,0:T(8,128)(2,1)S(1)} collective-permute-done((bf16[192,2048]{1,0:T(8,128)(2,1)}, bf16[192,2048]{1,0:T(8,128)(2,1)S(1)}, u32[]{:S(2)}, u32[]{:S(2)}) %collective-permute-start.43) | collective-permute-done | bytes 786464 | tf_op jit(solution)/shard_map/ppermute | solution.py:991
  (228 shorter events, 126.0 us)
Async XLA Ops:
  7.2 268.7 %all-reduce.4.cloned.1.call-start = ((), (), s32[]{:S(2)}) async-start(), calls=%async_computation | async-start | bytes 6291456 | tf_op jit(solution)/shard_map/psum | solution.py:1440
  13.2 11.2 %collective-permute-start.27 = (bf16[448,384]{1,0:T(8,128)(2,1)S(1)}, bf16[448,384]{1,0:T(8,128)(2,1)S(1)}, u32[]{:S(2)}, u32[]{:S(2)}) collective-permute-start(bf16[448,384]{1,0:T(8,128)(2,1)S(1)} %get-tuple-element.372.refs_1_), channel_id=1, source_target_pairs={{0,2},{1,3},{2,0},{3,1},{4,6},{5,7},{6,4},{7,5},{8,10},{9,11},{10,... | collective-permute-start | bytes 1032200 | tf_op jit(solution)/shard_map/ppermute | solution.py:947
  33.7 5.2 %collective-permute-start.29 = (bf16[448,384]{1,0:T(8,128)(2,1)S(1)}, bf16[448,384]{1,0:T(8,128)(2,1)S(1)}, u32[]{:S(2)}, u32[]{:S(2)}) collective-permute-start(bf16[448,384]{1,0:T(8,128)(2,1)S(1)} %get-tuple-element.382), channel_id=1, source_target_pairs={{0,1},{1,0},{2,3},{3,2},{4,5},{5,4},{6,7},{7,6},{8,9},{9,8},{10,11... | collective-permute-start | bytes 1032200 | tf_op jit(solution)/shard_map/ppermute | solution.py:947
  35.3 10.2 %collective-permute-start.31 = (bf16[448,384]{1,0:T(8,128)(2,1)S(1)}, bf16[448,384]{1,0:T(8,128)(2,1)S(1)}, u32[]{:S(2)}, u32[]{:S(2)}) collective-permute-start(bf16[448,384]{1,0:T(8,128)(2,1)S(1)} %add_convert_fusion.3), channel_id=1, source_target_pairs={{0,2},{1,3},{2,0},{3,1},{4,6},{5,7},{6,4},{7,5},{8,10},{9,11},{10,... | collective-permute-start | bytes 1032200 | tf_op jit(solution)/shard_map/ppermute | solution.py:947
  51.7 10.5 %collective-permute-start.33 = (bf16[448,384]{1,0:T(8,128)(2,1)S(1)}, bf16[448,384]{1,0:T(8,128)(2,1)S(1)}, u32[]{:S(2)}, u32[]{:S(2)}) collective-permute-start(bf16[448,384]{1,0:T(8,128)(2,1)S(1)} %get-tuple-element.386.refs_1_), channel_id=1, source_target_pairs={{0,2},{1,3},{2,0},{3,1},{4,6},{5,7},{6,4},{7,5},{8,10},{9,11},{10,... | collective-permute-start | bytes 1032200 | tf_op jit(solution)/shard_map/ppermute | solution.py:947
  72.7 10.2 %collective-permute-start.37 = (bf16[448,384]{1,0:T(8,128)(2,1)S(1)}, bf16[448,384]{1,0:T(8,128)(2,1)S(1)}, u32[]{:S(2)}, u32[]{:S(2)}) collective-permute-start(bf16[448,384]{1,0:T(8,128)(2,1)S(1)} %add_convert_fusion.2), channel_id=1, source_target_pairs={{0,2},{1,3},{2,0},{3,1},{4,6},{5,7},{6,4},{7,5},{8,10},{9,11},{10,... | collective-permute-start | bytes 1032200 | tf_op jit(solution)/shard_map/ppermute | solution.py:947
  99.8 12.0 %collective-permute-start.38 = (bf16[448,384]{1,0:T(8,128)(2,1)S(1)}, bf16[448,384]{1,0:T(8,128)(2,1)}, u32[]{:S(2)}, u32[]{:S(2)}) collective-permute-start(bf16[448,384]{1,0:T(8,128)(2,1)S(1)} %get-tuple-element.399.refs_1_), channel_id=1, source_target_pairs={{0,2},{1,3},{2,0},{3,1},{4,6},{5,7},{6,4},{7,5},{8,10},{9,11},{10,... | collective-permute-start | bytes 1032200 | tf_op jit(solution)/shard_map/ppermute | solution.py:947
  128.1 10.3 %collective-permute-start.1 = (bf16[448,384]{1,0:T(8,128)(2,1)S(1)}, bf16[448,384]{1,0:T(8,128)(2,1)S(1)}, u32[]{:S(2)}, u32[]{:S(2)}) collective-permute-start(bf16[448,384]{1,0:T(8,128)(2,1)S(1)} %get-tuple-element.102), channel_id=1, source_target_pairs={{0,1},{1,0},{2,3},{3,2},{4,5},{5,4},{6,7},{7,6},{8,9},{9,8},{10,11... | collective-permute-start | bytes 1032200 | tf_op jit(solution)/shard_map/cond/branch_1_fun/ppermute | solution.py:947
  129.7 11.9 %collective-permute-start.3 = (bf16[448,384]{1,0:T(8,128)(2,1)S(1)}, bf16[448,384]{1,0:T(8,128)(2,1)S(1)}, u32[]{:S(2)}, u32[]{:S(2)}) collective-permute-start(bf16[448,384]{1,0:T(8,128)(2,1)S(1)} %add_convert_fusion.1), channel_id=1, source_target_pairs={{0,2},{1,3},{2,0},{3,1},{4,6},{5,7},{6,4},{7,5},{8,10},{9,11},{10,... | collective-permute-start | bytes 1032200 | tf_op jit(solution)/shard_map/cond/branch_1_fun/ppermute | solution.py:947
  150.1 13.6 %collective-permute-start.5 = (bf16[448,384]{1,0:T(8,128)(2,1)S(1)}, bf16[448,384]{1,0:T(8,128)(2,1)S(1)}, u32[]{:S(2)}, u32[]{:S(2)}) collective-permute-start(bf16[448,384]{1,0:T(8,128)(2,1)S(1)} %get-tuple-element.147.refs_1_.refs_7_), channel_id=1, source_target_pairs={{0,2},{1,3},{2,0},{3,1},{4,6},{5,7},{6,4},{7,5},{8,10},{9,11},{10,... | collective-permute-start | bytes 1032200 | tf_op jit(solution)/shard_map/cond/branch_1_fun/ppermute | solution.py:947
  171.1 16.7 %collective-permute-start.8 = (bf16[192,2048]{1,0:T(8,128)(2,1)}, bf16[192,2048]{1,0:T(8,128)(2,1)S(1)}, u32[]{:S(2)}, u32[]{:S(2)}) collective-permute-start(bf16[192,2048]{1,0:T(8,128)(2,1)} %get-tuple-element.160), channel_id=1, source_target_pairs={{0,4},{1,9},{2,6},{3,11},{4,0},{5,13},{6,2},{7,15},{8,12},{9,1},{1... | collective-permute-start | bytes 2359304 | tf_op jit(solution)/shard_map/cond/branch_1_fun/ppermute | solution.py:991
  188.7 4.8 %collective-permute-start.10 = (bf16[448,384]{1,0:T(8,128)(2,1)}, bf16[448,384]{1,0:T(8,128)(2,1)S(1)}, u32[]{:S(2)}, u32[]{:S(2)}) collective-permute-start(bf16[448,384]{1,0:T(8,128)(2,1)} %get-tuple-element.164), channel_id=1, source_target_pairs={{0,1},{1,0},{2,3},{3,2},{4,5},{5,4},{6,7},{7,6},{8,9},{9,8},{10,11... | collective-permute-start | bytes 1032200 | tf_op jit(solution)/shard_map/cond/branch_1_fun/ppermute | solution.py:947
  188.9 6.6 %collective-permute-start.9 = (bf16[448,384]{1,0:T(8,128)(2,1)}, bf16[448,384]{1,0:T(8,128)(2,1)S(1)}, u32[]{:S(2)}, u32[]{:S(2)}) collective-permute-start(bf16[448,384]{1,0:T(8,128)(2,1)} %copy-done.17), channel_id=1, source_target_pairs={{0,1},{1,0},{2,3},{3,2},{4,5},{5,4},{6,7},{7,6},{8,9},{9,8},{10,11... | collective-permute-start | bytes 1032200 | tf_op jit(solution)/shard_map/cond/branch_1_fun/ppermute | solution.py:947
  191.6 9.1 %collective-permute-start.12 = (bf16[96,2048]{1,0:T(8,128)(2,1)}, bf16[96,2048]{1,0:T(8,128)(2,1)S(1)}, u32[]{:S(2)}, u32[]{:S(2)}) collective-permute-start(bf16[96,2048]{1,0:T(8,128)(2,1)} %get-tuple-element.174), channel_id=1, source_target_pairs={{0,8},{1,5},{2,10},{3,7},{4,12},{5,1},{6,14},{7,3},{8,0},{9,13},{1... | collective-permute-start | bytes 1179656 | tf_op jit(solution)/shard_map/cond/branch_1_fun/ppermute | solution.py:991
  193.6 11.8 %collective-permute-start.11 = (bf16[448,384]{1,0:T(8,128)(2,1)S(1)}, bf16[448,384]{1,0:T(8,128)(2,1)S(1)}, u32[]{:S(2)}, u32[]{:S(2)}) collective-permute-start(bf16[448,384]{1,0:T(8,128)(2,1)S(1)} %add_convert_fusion), channel_id=1, source_target_pairs={{0,2},{1,3},{2,0},{3,1},{4,6},{5,7},{6,4},{7,5},{8,10},{9,11},{10,... | collective-permute-start | bytes 1032200 | tf_op jit(solution)/shard_map/cond/branch_1_fun/ppermute | solution.py:947
  209.3 6.9 %collective-permute-start.13 = (bf16[48,2048]{1,0:T(8,128)(2,1)S(1)}, bf16[48,2048]{1,0:T(8,128)(2,1)S(1)}, u32[]{:S(2)}, u32[]{:S(2)}) collective-permute-start(bf16[48,2048]{1,0:T(8,128)(2,1)S(1)} %get-tuple-element.208), channel_id=1, source_target_pairs={{0,2},{1,3},{2,0},{3,1},{4,6},{5,7},{6,4},{7,5},{8,10},{9,11},{10,... | collective-permute-start | bytes 589832 | tf_op jit(solution)/shard_map/cond/branch_1_fun/ppermute | solution.py:991
  216.3 16.4 %collective-permute-start.14 = (bf16[192,2048]{1,0:T(8,128)(2,1)S(1)}, bf16[192,2048]{1,0:T(8,128)(2,1)S(1)}, u32[]{:S(2)}, u32[]{:S(2)}) collective-permute-start(bf16[192,2048]{1,0:T(8,128)(2,1)S(1)} %get-tuple-element.221), channel_id=1, source_target_pairs={{0,4},{1,9},{2,6},{3,11},{4,0},{5,13},{6,2},{7,15},{8,12},{9,1},{1... | collective-permute-start | bytes 2359304 | tf_op jit(solution)/shard_map/cond/branch_1_fun/ppermute | solution.py:991
  217.1 9.1 %collective-permute-start.15 = (bf16[48,1024]{1,0:T(8,128)(2,1)S(1)}, bf16[48,1024]{1,0:T(8,128)(2,1)S(1)}, u32[]{:S(2)}, u32[]{:S(2)}) collective-permute-start(bf16[48,1024]{1,0:T(8,128)(2,1)S(1)} %get-tuple-element.223), channel_id=1, source_target_pairs={{0,16},{1,17},{2,18},{3,19},{4,20},{5,21},{6,22},{7,23},{8,24},{9,... | collective-permute-start | bytes 294920 | tf_op jit(solution)/shard_map/cond/branch_1_fun/ppermute | solution.py:991
  236.0 12.2 %collective-permute-start.17 = (bf16[96,2048]{1,0:T(8,128)(2,1)}, bf16[96,2048]{1,0:T(8,128)(2,1)S(1)}, u32[]{:S(2)}, u32[]{:S(2)}) collective-permute-start(bf16[96,2048]{1,0:T(8,128)(2,1)} %get-tuple-element.235), channel_id=1, source_target_pairs={{0,8},{1,5},{2,10},{3,7},{4,12},{5,1},{6,14},{7,3},{8,0},{9,13},{1... | collective-permute-start | bytes 1179656 | tf_op jit(solution)/shard_map/cond/branch_1_fun/ppermute | solution.py:991
  237.3 8.8 %collective-permute-start.18 = (bf16[48,1024]{1,0:T(8,128)(2,1)S(1)}, bf16[48,1024]{1,0:T(8,128)(2,1)S(1)}, u32[]{:S(2)}, u32[]{:S(2)}) collective-permute-start(bf16[48,1024]{1,0:T(8,128)(2,1)S(1)} %fold.12.own), channel_id=1, source_target_pairs={{0,16},{1,17},{2,18},{3,19},{4,20},{5,21},{6,22},{7,23},{8,24},{9,... | collective-permute-start | bytes 294920 | tf_op jit(solution)/shard_map/cond/branch_1_fun/ppermute | solution.py:991
  246.2 9.5 %collective-permute-start.21 = (bf16[48,2048]{1,0:T(8,128)(2,1)S(1)}, bf16[48,2048]{1,0:T(8,128)(2,1)S(1)}, u32[]{:S(2)}, u32[]{:S(2)}) collective-permute-start(bf16[48,2048]{1,0:T(8,128)(2,1)S(1)} %join.5.own), channel_id=1, source_target_pairs={{0,2},{1,3},{2,0},{3,1},{4,6},{5,7},{6,4},{7,5},{8,10},{9,11},{10,... | collective-permute-start | bytes 589832 | tf_op jit(solution)/shard_map/cond/branch_1_fun/ppermute | solution.py:991
  250.1 5.5 %collective-permute-start.22 = (f32[56,384]{1,0:T(8,128)S(1)}, f32[56,384]{1,0:T(8,128)S(1)}, u32[]{:S(2)}, u32[]{:S(2)}) collective-permute-start(f32[56,384]{1,0:T(8,128)S(1)} %add.27), channel_id=1, source_target_pairs={{0,4},{1,9},{2,6},{3,11},{4,0},{5,13},{6,2},{7,15},{8,12},{9,1},{1... | collective-permute-start | bytes 258056 | tf_op jit(solution)/shard_map/cond/branch_1_fun/ppermute | solution.py:991
  251.5 8.6 %collective-permute-start.20 = (bf16[48,2048]{1,0:T(8,128)(2,1)S(1)}, bf16[48,2048]{1,0:T(8,128)(2,1)S(1)}, u32[]{:S(2)}, u32[]{:S(2)}) collective-permute-start(bf16[48,2048]{1,0:T(8,128)(2,1)S(1)} %get-tuple-element.249), channel_id=1, source_target_pairs={{0,16},{1,17},{2,18},{3,19},{4,20},{5,21},{6,22},{7,23},{8,24},{9,... | collective-permute-start | bytes 589832 | tf_op jit(solution)/shard_map/cond/branch_1_fun/ppermute | solution.py:991
  256.5 15.5 %collective-permute-start.24 = (bf16[96,2048]{1,0:T(8,128)(2,1)}, bf16[96,2048]{1,0:T(8,128)(2,1)S(1)}, u32[]{:S(2)}, u32[]{:S(2)}) collective-permute-start(bf16[96,2048]{1,0:T(8,128)(2,1)} %join.6.own), channel_id=1, source_target_pairs={{0,8},{1,5},{2,10},{3,7},{4,12},{5,1},{6,14},{7,3},{8,0},{9,13},{1... | collective-permute-start | bytes 1179656 | tf_op jit(solution)/shard_map/cond/branch_1_fun/ppermute | solution.py:991
  260.2 12.5 %collective-permute-start.23 = (bf16[48,2048]{1,0:T(8,128)(2,1)S(1)}, bf16[48,2048]{1,0:T(8,128)(2,1)S(1)}, u32[]{:S(2)}, u32[]{:S(2)}) collective-permute-start(bf16[48,2048]{1,0:T(8,128)(2,1)S(1)} %fold.15.own), channel_id=1, source_target_pairs={{0,16},{1,17},{2,18},{3,19},{4,20},{5,21},{6,22},{7,23},{8,24},{9,... | collective-permute-start | bytes 589832 | tf_op jit(solution)/shard_map/cond/branch_1_fun/ppermute | solution.py:991
  261.3 10.0 %collective-permute-start.25 = (f32[56,384]{1,0:T(8,128)S(1)}, f32[56,384]{1,0:T(8,128)S(1)}, u32[]{:S(2)}, u32[]{:S(2)}) collective-permute-start(f32[56,384]{1,0:T(8,128)S(1)} %add.28), channel_id=1, source_target_pairs={{0,8},{1,5},{2,10},{3,7},{4,12},{5,1},{6,14},{7,3},{8,0},{9,13},{1... | collective-permute-start | bytes 258056 | tf_op jit(solution)/shard_map/cond/branch_1_fun/ppermute | solution.py:991
  275.9 16.4 %collective-permute-start.40 = (bf16[192,2048]{1,0:T(8,128)(2,1)}, bf16[192,2048]{1,0:T(8,128)(2,1)S(1)}, u32[]{:S(2)}, u32[]{:S(2)}) collective-permute-start(bf16[192,2048]{1,0:T(8,128)(2,1)} %get-tuple-element.434.refs_0_), channel_id=1, source_target_pairs={{0,4},{1,9},{2,6},{3,11},{4,0},{5,13},{6,2},{7,15},{8,12},{9,1},{1... | collective-permute-start | bytes 2359304 | tf_op jit(solution)/shard_map/ppermute | solution.py:991
  277.5 19.5 %collective-permute-start.42 = (bf16[96,2048]{1,0:T(8,128)(2,1)}, bf16[96,2048]{1,0:T(8,128)(2,1)S(1)}, u32[]{:S(2)}, u32[]{:S(2)}) collective-permute-start(bf16[96,2048]{1,0:T(8,128)(2,1)} %get-tuple-element.444.own), channel_id=1, source_target_pairs={{0,8},{1,5},{2,10},{3,7},{4,12},{5,1},{6,14},{7,3},{8,0},{9,13},{1... | collective-permute-start | bytes 1179656 | tf_op jit(solution)/shard_map/ppermute | solution.py:991
  280.0 11.4 %collective-permute-start.41 = (f32[56,384]{1,0:T(8,128)}, f32[56,384]{1,0:T(8,128)S(1)}, u32[]{:S(2)}, u32[]{:S(2)}) collective-permute-start(f32[56,384]{1,0:T(8,128)} %get-tuple-element.439), channel_id=1, source_target_pairs={{0,16},{1,17},{2,18},{3,19},{4,20},{5,21},{6,22},{7,23},{8,24},{9,... | collective-permute-start | bytes 258056 | tf_op jit(solution)/shard_map/ppermute | solution.py:991
  280.2 20.7 %collective-permute-start.44 = (bf16[192,2048]{1,0:T(8,128)(2,1)}, bf16[192,2048]{1,0:T(8,128)(2,1)S(1)}, u32[]{:S(2)}, u32[]{:S(2)}) collective-permute-start(bf16[192,2048]{1,0:T(8,128)(2,1)} %get-tuple-element.434.refs_0_), channel_id=1, source_target_pairs={{0,1},{1,0},{2,3},{3,2},{4,5},{5,4},{6,7},{7,6},{8,9},{9,8},{10,11... | collective-permute-start | bytes 2359304 | tf_op jit(solution)/shard_map/ppermute | solution.py:991
  292.3 8.7 %collective-permute-start.45 = (bf16[192,2048]{1,0:T(8,128)(2,1)S(1)}, bf16[192,2048]{1,0:T(8,128)(2,1)S(1)}, u32[]{:S(2)}, u32[]{:S(2)}) collective-permute-start(bf16[192,2048]{1,0:T(8,128)(2,1)S(1)} %collective-permute-done.40.refs_1_), channel_id=1, source_target_pairs={{0,1},{1,0},{2,3},{3,2},{4,5},{5,4},{6,7},{7,6},{8,9},{9,8},{10,11... | collective-permute-start | bytes 2359304 | tf_op jit(solution)/shard_map/ppermute | solution.py:991
  299.8 12.2 %collective-permute-start.43 = (bf16[192,2048]{1,0:T(8,128)(2,1)}, bf16[192,2048]{1,0:T(8,128)(2,1)S(1)}, u32[]{:S(2)}, u32[]{:S(2)}) collective-permute-start(bf16[192,2048]{1,0:T(8,128)(2,1)} %join.9.refs_0_), channel_id=1, source_target_pairs={{0,4},{1,9},{2,6},{3,11},{4,0},{5,13},{6,2},{7,15},{8,12},{9,1},{1... | collective-permute-start | bytes 2359304 | tf_op jit(solution)/shard_map/ppermute | solution.py:991
  (71 other events, 736.8 us)
Sparse Core Ops, SparseCore 0:
  99.9 146.1 all-reduce.3
